TPU v7x, 32 devices: a whole 2x2x4 slice. The times are simulated.
32 devices in a mesh: fsdp: 8 (over z, core), ctx: 4 (over y, x).
Axes of the slice: x: 2, y: 2, z: 4, core: 2. Of those that a mesh axis runs over, the one named last changes fastest.
Arguments:
- tokens: bfloat16 [8, 4096, 1088], P('fsdp', 'ctx'), may hold values from -6 to 6
- cotangent: bfloat16 [8, 4096, 1088], P('fsdp', 'ctx'), may hold values from -6 to 6
- lengths: int32 [8], P('fsdp'), may hold values from 1024 to 4096, as said below
- block_order: int32 [8, 8], P('fsdp'), may hold values from 0 to 7, each once within a row
- ln1_gain: float32 [2, 1088], P(None, 'fsdp'), may hold values from 0.25 to 1.75
- ln1_bias: float32 [2, 1088], P(None, 'fsdp'), may hold values from -1 to 1
- qkv_weight: float32 [2, 1088, 3264], P(None, 'fsdp'), may hold values from -0.1875 to 0.1875
- q_bias: float32 [2, 1088], P(None, 'fsdp'), may hold values from -1.5 to 1.5
- v_bias: float32 [2, 1088], P(None, 'fsdp'), may hold values from -1.5 to 1.5
- out_weight: float32 [2, 1088, 1088], P(None, 'fsdp'), may hold values from -1.5 to 1.5
- out_bias: float32 [2, 1088], P(None, 'fsdp'), may hold values from -1 to 1
- ln2_gain: float32 [2, 1088], P(None, 'fsdp'), may hold values from 0.25 to 1.75
- ln2_bias: float32 [2, 1088], P(None, 'fsdp'), may hold values from -1 to 1
- up_weight: float32 [2, 1088, 4352], P(None, 'fsdp'), may hold values from -0.1875 to 0.1875
- up_bias: float32 [2, 4352], P(None, 'fsdp'), may hold values from -1.5 to 1.5
- down_weight: float32 [2, 4352, 1088], P(None, 'fsdp'), may hold values from -0.09375 to 0.09375
- down_bias: float32 [2, 1088], P(None, 'fsdp'), may hold values from -1 to 1
Outputs:
- activations: bfloat16 [8, 4096, 1088], P('fsdp', 'ctx')
- tokens_grad: float32 [8, 4096, 1088], P('fsdp', 'ctx')
- ln1_gain_grad: float32 [2, 1088], P(None, 'fsdp')
- ln1_bias_grad: float32 [2, 1088], P(None, 'fsdp')
- qkv_weight_grad: float32 [2, 1088, 3264], P(None, 'fsdp')
- q_bias_grad: float32 [2, 1088], P(None, 'fsdp')
- v_bias_grad: float32 [2, 1088], P(None, 'fsdp')
- out_weight_grad: float32 [2, 1088, 1088], P(None, 'fsdp')
- out_bias_grad: float32 [2, 1088], P(None, 'fsdp')
- ln2_gain_grad: float32 [2, 1088], P(None, 'fsdp')
- ln2_bias_grad: float32 [2, 1088], P(None, 'fsdp')
- up_weight_grad: float32 [2, 1088, 4352], P(None, 'fsdp')
- up_bias_grad: float32 [2, 4352], P(None, 'fsdp')
- down_weight_grad: float32 [2, 4352, 1088], P(None, 'fsdp')
- down_bias_grad: float32 [2, 1088], P(None, 'fsdp')
Inputs may be any that keep to these rules, and one draw needn't show every extreme that they name: Some slot holds exactly 4096 valid tokens and some exactly 1024; valid tokens are the first lengths of the sequence positions. `block_order`: each row names every block of its slot once.
All inputs are finite; a program needn't handle non-finite values.
Results may differ from a plain program's by a relative error of at most 0.019.
Values may be sent and summed in bfloat16 or wider, within the bound.
A program may use at most 512 MiB of HBM per device.

v0:
```python
import functools
import jax, jax.numpy as jnp
from jax import lax
from jax.experimental import pallas as pl
from jax.experimental.pallas import tpu as pltpu
from jax.experimental.layout import Layout, with_layout_constraint
from jax.sharding import Mesh, PartitionSpec as P
f32=jnp.float32; bf16=jnp.bfloat16
NEG=-1e30
def dot_nt(a,b): return lax.dot_general(a,b,(((1,),(1,)),((),())),preferred_element_type=f32)
def dot_nn(a,b): return lax.dot_general(a,b,(((1,),(0,)),((),())),preferred_element_type=f32)

LOG2E=1.4426950408889634
def split(q,h,low):
    qs=q.astype(f32)*(0.125*LOG2E)
    hi=qs.astype(bf16).astype(f32); lo=qs-hi
    rl=pltpu.roll(lo,64,1)
    c=jnp.where(low,hi,rl) if h==0 else jnp.where(low,rl,hi)
    return c.astype(bf16)
def dup(k,h,low):
    kf=k.astype(f32); rl=pltpu.roll(kf,64,1)
    c=jnp.where(low,kf,rl) if h==0 else jnp.where(low,rl,kf)
    return c.astype(bf16)
def fwd_kernel(inv_ref, nb_ref, x_ref, o_ref, lse_ref, vt, kd, sb, acc, *, B, NB):
    s=pl.program_id(0)
    nb=nb_ref[s]
    lane=lax.broadcasted_iota(jnp.int32,(1,128),1)
    low=lane<64
    def tv(j,_):
        r=pl.multiple_of(inv_ref[s,j]*B,B)
        w=pl.multiple_of(j*B,B)
        t=x_ref[0,pl.ds(r,B),256:384].T
        one=(lax.broadcasted_iota(jnp.int32,(16,B),0)==0).astype(bf16)
        for h in range(2):
            vt[80*h:80*h+64,pl.ds(w,B)]=t[64*h:64*h+64,:]
            vt[80*h+64:80*h+80,pl.ds(w,B)]=one
            kd[h,pl.ds(w,B),:]=dup(x_ref[0,pl.ds(r,B),128:256],h,low)
        return 0
    lax.fori_loop(0,nb,tv,0)
    rr=lax.broadcasted_iota(jnp.int32,(B,B),0)
    cc=lax.broadcasted_iota(jnp.int32,(B,B),1)
    def qblock(i,_):
        r=pl.multiple_of(inv_ref[s,i]*B,B)
        q=x_ref[0,pl.ds(r,B),0:128]
        qh=[split(q,h,low) for h in range(2)]
        acc[...]=jnp.zeros_like(acc)
        def scores(j,slot):
            for h in range(2):
                sb[slot,h]=dot_nt(kd[h,pl.ds(pl.multiple_of(j*B,B),B),:],qh[h])
        def step(j,carry,diag):
            out=[]
            for h in range(2):
                m=carry[h]
                st=sb[j%2,h]
                if diag: st=jnp.where(rr<=cc,st,NEG)
                mn=jnp.maximum(m,jnp.max(st,axis=0,keepdims=True))
                p=jnp.exp2(st-mn)
                al=jnp.exp2(m-mn)
                v=vt[80*h:80*h+80,pl.ds(pl.multiple_of(j*B,B),B)]
                acc[h]=acc[h]*al+dot_nn(v,p.astype(bf16))
                out.append(mn)
            return tuple(out)
        scores(0,0)
        def both(j,c):
            scores(j+1,(j+1)%2)
            return step(j,c,False)
        n=jnp.full((1,B),NEG,f32)
        c=lax.fori_loop(0,i,both,(n,n))
        c=step(i,c,True)
        os=[]
        for h in range(2):
            l=acc[h,64:65,:]
            os.append(acc[h,0:64,:]*(1.0/l))
            lse_ref[0,pl.ds(h,1),pl.ds(r,B)]=c[h]+jnp.log2(l)
        o_ref[0,pl.ds(r,B),:]=jnp.concatenate(os,0).T.astype(bf16)
        return 0
    lax.fori_loop(0,nb,qblock,0)
    def pad(i,_):
        r=pl.multiple_of(inv_ref[s,i]*B,B)
        o_ref[0,pl.ds(r,B),:]=jnp.zeros((B,128),bf16)
        lse_ref[0,:,pl.ds(r,B)]=jnp.zeros((8,B),f32)
        return 0
    lax.fori_loop(nb,NB,pad,0)

def flash_fwd(x,inv,nb,B):
    S,N,_=x.shape
    NB=N//B
    return pl.pallas_call(functools.partial(fwd_kernel,B=B,NB=NB),
      out_shape=(jax.ShapeDtypeStruct((S,N,128),bf16),jax.ShapeDtypeStruct((S,8,N),f32)),
      grid_spec=pltpu.PrefetchScalarGridSpec(num_scalar_prefetch=2,grid=(S,),
        in_specs=[pl.BlockSpec((1,N,384),lambda s,*_:(s,0,0))],
        out_specs=[pl.BlockSpec((1,N,128),lambda s,*_:(s,0,0)),pl.BlockSpec((1,8,N),lambda s,*_:(s,0,0))],
        scratch_shapes=[pltpu.VMEM((160,N),bf16),pltpu.VMEM((2,N,128),bf16),pltpu.VMEM((2,2,B,B),f32),pltpu.VMEM((2,80,B),f32)]),
      compiler_params=pltpu.CompilerParams(vmem_limit_bytes=48<<20),
      cost_estimate=pl.CostEstimate(flops=S*4*N*N*128,bytes_accessed=S*N*1024,transcendentals=S*N*N),
      )(inv,nb,x)

def bwd_kernel(inv_ref, nb_ref, x_ref, o_ref, do_ref, lse_ref, dx_ref, kt, qd, dq, dk, dv, dl, *, B, NB):
    s=pl.program_id(0)
    nb=nb_ref[s]
    lane=lax.broadcasted_iota(jnp.int32,(1,128),1)
    low=lane<64
    hm=(lax.broadcasted_iota(jnp.int32,(8,128),1)//64==lax.broadcasted_iota(jnp.int32,(8,128),0)).astype(bf16)
    def prep(j,_):
        r=pl.multiple_of(inv_ref[s,j]*B,B)
        w=pl.multiple_of(j*B,B)
        kt[:,pl.ds(w,B)]=x_ref[0,pl.ds(r,B),128:256].T
        for h in range(2): qd[h,pl.ds(w,B),:]=split(x_ref[0,pl.ds(r,B),0:128],h,low)
        prod=o_ref[0,pl.ds(r,B),:].astype(f32)*do_ref[0,pl.ds(r,B),:].astype(f32)
        hi=prod.astype(bf16); lo=(prod-hi.astype(f32)).astype(bf16)
        dl[:,pl.ds(w,B)]=dot_nt(hm,hi)+dot_nt(hm,lo)
        dq[:,pl.ds(w,B)]=jnp.zeros((128,B),f32)
        return 0
    lax.fori_loop(0,nb,prep,0)
    rr=lax.broadcasted_iota(jnp.int32,(B,B),0)
    cc=lax.broadcasted_iota(jnp.int32,(B,B),1)
    def kblock(j,_):
        r=pl.multiple_of(inv_ref[s,j]*B,B)
        k=x_ref[0,pl.ds(r,B),128:256]
        v=x_ref[0,pl.ds(r,B),256:384]
        kdh=[dup(k,h,low) for h in range(2)]
        dk[...]=jnp.zeros_like(dk); dv[...]=jnp.zeros_like(dv)
        def step(i,diag):
            ri=pl.multiple_of(inv_ref[s,i]*B,B)
            wi=pl.multiple_of(i*B,B)
            q=x_ref[0,pl.ds(ri,B),0:128]*jnp.asarray(0.125,bf16)
            do=do_ref[0,pl.ds(ri,B),:]
            zero=jnp.zeros_like(q)
            dvs=[];dks=[]
            for h in range(2):
                qh=jnp.where(low,q,zero) if h==0 else jnp.where(low,zero,q)
                doh=jnp.where(low,do,zero) if h==0 else jnp.where(low,zero,do)
                st=dot_nt(kdh[h],qd[h,pl.ds(wi,B),:])
                p=jnp.exp2(st-lse_ref[0,pl.ds(h,1),pl.ds(ri,B)])
                if diag: p=jnp.where(rr<=cc,p,0.0)
                dvs.append(dot_nn(p.astype(bf16),doh))
                dp=dot_nt(v,doh)
                ds=(p*(dp-dl[pl.ds(h,1),pl.ds(wi,B)])).astype(bf16)
                dks.append(dot_nn(ds,qh))
                kh=kt[64*h:64*h+64,pl.ds(pl.multiple_of(j*B,B),B)]
                dq[64*h:64*h+64,pl.ds(wi,B)]+=dot_nn(kh,ds)
            dv[...]+=dvs[0]+dvs[1]
            dk[...]+=dks[0]+dks[1]
        step(j,True)
        def body(i,_):
            step(i,False); return 0
        lax.fori_loop(j+1,nb,body,0)
        dx_ref[0,pl.ds(r,B),128:256]=dk[...].astype(bf16)
        dx_ref[0,pl.ds(r,B),256:384]=dv[...].astype(bf16)
        return 0
    lax.fori_loop(0,nb,kblock,0)
    def fin(i,_):
        r=pl.multiple_of(inv_ref[s,i]*B,B)
        dx_ref[0,pl.ds(r,B),0:128]=(dq[:,pl.ds(pl.multiple_of(i*B,B),B)].T*0.125).astype(bf16)
        return 0
    lax.fori_loop(0,nb,fin,0)
    def pad(i,_):
        r=pl.multiple_of(inv_ref[s,i]*B,B)
        dx_ref[0,pl.ds(r,B),:]=jnp.zeros((B,384),bf16)
        return 0
    lax.fori_loop(nb,NB,pad,0)

def flash_bwd(x,o,do,lse,inv,nb,B):
    S,N,_=x.shape
    NB=N//B
    return pl.pallas_call(functools.partial(bwd_kernel,B=B,NB=NB),
      out_shape=jax.ShapeDtypeStruct((S,N,384),bf16),
      grid_spec=pltpu.PrefetchScalarGridSpec(num_scalar_prefetch=2,grid=(S,),
        in_specs=[pl.BlockSpec((1,N,384),lambda s,*_:(s,0,0)),pl.BlockSpec((1,N,128),lambda s,*_:(s,0,0)),
                  pl.BlockSpec((1,N,128),lambda s,*_:(s,0,0)),pl.BlockSpec((1,8,N),lambda s,*_:(s,0,0))],
        out_specs=pl.BlockSpec((1,N,384),lambda s,*_:(s,0,0)),
        scratch_shapes=[pltpu.VMEM((128,N),bf16),pltpu.VMEM((2,N,128),bf16),pltpu.VMEM((128,N),f32),pltpu.VMEM((B,128),f32),pltpu.VMEM((B,128),f32),pltpu.VMEM((8,N),f32)]),
      compiler_params=pltpu.CompilerParams(vmem_limit_bytes=48<<20),
      cost_estimate=pl.CostEstimate(flops=S*10*N*N*128,bytes_accessed=S*N*2400,transcendentals=S*N*N),
      )(inv,nb,x,o,do,lse)


def one_fwd_kernel(own_ref, q_ref, x_ref, o_ref, lse_ref, vt, kd, acc, *, B, NB):
    nb = own_ref[NB + 2]
    low = lax.broadcasted_iota(jnp.int32,(1,128),1)<64
    def tv(j,_):
        r=pl.multiple_of(own_ref[j]*B,B)
        t=x_ref[pl.ds(r,B),:].T
        w=pl.multiple_of(j*B,B)
        kd[pl.ds(w,B),:]=dup(x_ref[pl.ds(r,B),:],0,low)
        vt[0:64,pl.ds(w,B)]=t[64:128,:]
        vt[64:80,pl.ds(w,B)]=(lax.broadcasted_iota(jnp.int32,(16,B),0)==0).astype(bf16)
        return 0
    lax.fori_loop(0,nb,tv,0)
    rr=lax.broadcasted_iota(jnp.int32,(B,B),0)
    cc=lax.broadcasted_iota(jnp.int32,(B,B),1)
    for t in range(2):
        i=own_ref[NB+t]
        @pl.when(i>=nb)
        def _():
            o_ref[t*B:(t+1)*B,:]=jnp.zeros((B,64),bf16)
            lse_ref[:,t*B:(t+1)*B]=jnp.zeros((8,B),f32)
        @pl.when(i<nb)
        def _():
            qs=q_ref[t*B:(t+1)*B,:].astype(f32)*(0.125*LOG2E)
            hi=qs.astype(bf16)
            q=jnp.concatenate([hi.astype(f32),qs-hi.astype(f32)],axis=1).astype(bf16)
            acc[...]=jnp.zeros_like(acc)
            def step(j,m,diag):
                st=dot_nt(kd[pl.ds(pl.multiple_of(j*B,B),B),:],q)
                if diag: st=jnp.where(rr<=cc,st,NEG)
                mn=jnp.maximum(m,jnp.max(st,axis=0,keepdims=True))
                p=jnp.exp2(st-mn)
                al=jnp.exp2(m-mn)
                v=vt[:,pl.ds(pl.multiple_of(j*B,B),B)]
                acc[...]=acc[...]*al+dot_nn(v,p.astype(bf16))
                return mn
            m=lax.fori_loop(0,i,lambda j,m: step(j,m,False),jnp.full((1,B),NEG,f32))
            m=step(i,m,True)
            l=acc[64:65,:]
            o_ref[t*B:(t+1)*B,:]=(acc[0:64,:]*(1.0/l)).T.astype(bf16)
            lse_ref[:,t*B:(t+1)*B]=jnp.broadcast_to(m+jnp.log2(l),(8,B))


def one_fwd(q,x,own,B):
    N=x.shape[0]; R=q.shape[0]; NB=N//B
    full=lambda *_:(0,0)
    last=lambda *_:(0,3)
    return pl.pallas_call(functools.partial(one_fwd_kernel,B=B,NB=NB),
      out_shape=(jax.ShapeDtypeStruct((R,64),bf16),jax.ShapeDtypeStruct((8,R),f32)),
      grid_spec=pltpu.PrefetchScalarGridSpec(num_scalar_prefetch=1,grid=(1,),
        in_specs=[pl.BlockSpec((R,64),full),pl.BlockSpec((N,128),last)],
        out_specs=[pl.BlockSpec((R,64),full),pl.BlockSpec((8,R),full)],
        scratch_shapes=[pltpu.VMEM((80,N),bf16),pltpu.VMEM((N,128),bf16),pltpu.VMEM((80,B),f32)]),
      compiler_params=pltpu.CompilerParams(vmem_limit_bytes=48<<20),
      cost_estimate=pl.CostEstimate(flops=4*R*N*128,bytes_accessed=N*256+R*512,transcendentals=R*N),
      )(own,q,x)


def one_bwd_kernel(own_ref, q_ref, x_ref, o_ref, do_ref, lse_ref, dq_ref, dx_ref, dkv, dq, *, B, NB):
    nb = own_ref[NB + 2]
    low = lax.broadcasted_iota(jnp.int32,(1,128),1)<64
    rr=lax.broadcasted_iota(jnp.int32,(B,B),0)
    cc=lax.broadcasted_iota(jnp.int32,(B,B),1)
    ones=jnp.ones((8,64),bf16)
    dkv[...]=jnp.zeros_like(dkv)
    for t in range(2):
        i=own_ref[NB+t]
        sl=slice(t*B,(t+1)*B)
        @pl.when(i>=nb)
        def _():
            dq_ref[sl,:]=jnp.zeros((B,64),bf16)
        @pl.when(i<nb)
        def _():
            qr=q_ref[sl,:]
            qs=qr.astype(f32)*(0.125*LOG2E)
            hi=qs.astype(bf16)
            q=jnp.concatenate([hi.astype(f32),qs-hi.astype(f32)],axis=1).astype(bf16)
            qd=qr*jnp.asarray(0.125,bf16)
            do=do_ref[sl,:]
            prod=o_ref[sl,:].astype(f32)*do.astype(f32)
            hi=prod.astype(bf16); lo=(prod-hi.astype(f32)).astype(bf16)
            dl=(dot_nt(ones,hi)+dot_nt(ones,lo))[0:1,:]
            lse=lse_ref[0:1,sl]
            dq[...]=jnp.zeros_like(dq)
            def step(j,diag):
                r=pl.multiple_of(own_ref[j]*B,B)
                k=x_ref[pl.ds(r,B),0:64]
                v=x_ref[pl.ds(r,B),64:128]
                st=dot_nt(dup(x_ref[pl.ds(r,B),:],0,low),q)
                p=jnp.exp2(st-lse)
                if diag: p=jnp.where(rr<=cc,p,0.0)
                dp=dot_nt(v,do)
                ds=(p*(dp-dl)).astype(bf16)
                dkv[pl.ds(r,B),64:128]+=dot_nn(p.astype(bf16),do)
                dkv[pl.ds(r,B),0:64]+=dot_nn(ds,qd)
                dq[...]+=dot_nn(k.T,ds)
            def body(j,_):
                step(j,False); return 0
            lax.fori_loop(0,i,body,0)
            step(i,True)
            dq_ref[sl,:]=(dq[...].T*0.125).astype(bf16)
    dx_ref[...]=dkv[...].astype(bf16)


def one_bwd(q,x,o,do,lse,own,B):
    N=x.shape[0]; R=q.shape[0]; NB=N//B
    full=lambda *_:(0,0)
    last=lambda *_:(0,3)
    return pl.pallas_call(functools.partial(one_bwd_kernel,B=B,NB=NB),
      out_shape=(jax.ShapeDtypeStruct((R,64),bf16),jax.ShapeDtypeStruct((N,128),bf16)),
      grid_spec=pltpu.PrefetchScalarGridSpec(num_scalar_prefetch=1,grid=(1,),
        in_specs=[pl.BlockSpec((R,64),full),pl.BlockSpec((N,128),last),pl.BlockSpec((R,64),full),pl.BlockSpec((R,64),full),pl.BlockSpec((8,R),full)],
        out_specs=[pl.BlockSpec((R,64),full),pl.BlockSpec((N,128),full)],
        scratch_shapes=[pltpu.VMEM((N,128),f32),pltpu.VMEM((64,B),f32)]),
      compiler_params=pltpu.CompilerParams(vmem_limit_bytes=48<<20),
      cost_estimate=pl.CostEstimate(flops=10*R*N*128,bytes_accessed=N*512+R*1024,transcendentals=R*N),
      )(own,q,x,o,do,lse)


def join_kernel(*refs, count):
    t = pl.program_id(0)
    stacks, tail, out = refs[:-2], refs[-2], refs[-1]
    for i, ref in enumerate(stacks):
        @pl.when((t >= i * count) & (t < (i + 1) * count))
        def _(ref=ref):
            out[...] = ref[0]

    @pl.when(t >= len(stacks) * count)
    def _():
        out[:, :tail.shape[1]] = tail[...]


def join(stacks, tail):
    C, R, W = stacks[0].shape
    n = len(stacks)
    T = tail.shape[1]

    def at(i):
        return lambda t: (jnp.clip(t - i * C, 0, C - 1), 0, 0)
    return pl.pallas_call(functools.partial(join_kernel, count=C),
        out_shape=jax.ShapeDtypeStruct((R, n * C * W + T), bf16),
        grid=(n * C + 1,),
        in_specs=[pl.BlockSpec((1, R, W), at(i)) for i in range(n)] + [pl.BlockSpec((R, T), lambda t: (0, 0))],
        out_specs=pl.BlockSpec((R, W), lambda t: (0, t)),
        compiler_params=pltpu.CompilerParams(vmem_limit_bytes=56 << 20),
        cost_estimate=pl.CostEstimate(flops=0, bytes_accessed=4 * R * (n * C * W + T), transcendentals=0),
    )(*stacks, tail)


def deal_kernel(x_ref, o_ref):
    o_ref[0] = x_ref[...]


def deal(x, first, C, W):
    R = x.shape[0]
    return pl.pallas_call(deal_kernel,
        out_shape=jax.ShapeDtypeStruct((C, R, W), bf16),
        grid=(C,),
        in_specs=[pl.BlockSpec((R, W), lambda t: (0, first + t))],
        out_specs=pl.BlockSpec((1, R, W), lambda t: (t, 0, 0)),
        compiler_params=pltpu.CompilerParams(vmem_limit_bytes=56 << 20),
        cost_estimate=pl.CostEstimate(flops=0, bytes_accessed=4 * R * C * W, transcendentals=0),
    )(x)


def gather_kernel(x_ref, o_ref, own_sem, zs, zr, xs, xr, cs, cr, *, Z, C, quarter):
    z, a, c = lax.axis_index("zz"), lax.axis_index("core"), lax.axis_index("ctx")
    mesh_id = pl.DeviceIdType.MESH
    other = 1 - a
    peers = [(lax.rem(z + k, Z), a, c) for k in range(1, Z)] + [(z, a, lax.rem(c + j, C)) for j in range(1, C)] + [(z, other, c)]
    barrier = pltpu.get_barrier_semaphore()
    for peer in peers:
        pl.semaphore_signal(barrier, inc=1, device_id=peer, device_id_type=mesh_id)
    pl.semaphore_wait(barrier, len(peers))

    f = 2 * z + a

    def cols(q):
        return pl.ds(pl.multiple_of(q * quarter, quarter), quarter)

    def send(src, dst, s, r, peer):
        copy = pltpu.make_async_remote_copy(src_ref=src, dst_ref=dst, send_sem=s, recv_sem=r, device_id=peer, device_id_type=mesh_id)
        copy.start()
        return copy

    along = []
    for k in range(1, Z):
        along.append(send(x_ref.at[:, cols(c)], o_ref.at[f, :, cols(c)], zs.at[k - 1], zr.at[k - 1], peers[k - 1]))
    own = pltpu.make_async_copy(x_ref, o_ref.at[f], own_sem)
    own.start()
    whole = send(x_ref, o_ref.at[f], cs.at[0], cr.at[0], peers[-1])
    plane, cross = [], []
    for k in range(1, Z):
        along[k - 1].wait_recv()
        fs = 2 * lax.rem(z + Z - k, Z) + a
        piece = o_ref.at[fs, :, cols(c)]
        for j in range(1, C):
            n = (k - 1) * (C - 1) + j - 1
            plane.append(send(piece, piece, xs.at[n], xr.at[n], peers[Z - 1 + j - 1]))
        n = 1 + (k - 1) * C
        cross.append(send(piece, piece, cs.at[n], cr.at[n], peers[-1]))
    for k in range(1, Z):
        fs = 2 * lax.rem(z + Z - k, Z) + a
        for j in range(1, C):
            plane[(k - 1) * (C - 1) + j - 1].wait_recv()
            piece = o_ref.at[fs, :, cols(lax.rem(c + C - j, C))]
            n = 1 + (k - 1) * C + j
            cross.append(send(piece, piece, cs.at[n], cr.at[n], peers[-1]))
    for copy in along + plane:
        copy.wait_send()
    whole.wait_send()
    whole.wait_recv()
    for copy in cross:
        copy.wait_send()
        copy.wait_recv()
    own.wait()


def gather_all(x, Z, C):
    R, W = x.shape
    dma = pltpu.SemaphoreType.DMA
    n, m = (Z - 1) * (C - 1), 1 + (Z - 1) * C
    return pl.pallas_call(functools.partial(gather_kernel, Z=Z, C=C, quarter=W // C),
        out_shape=jax.ShapeDtypeStruct((2 * Z, R, W), bf16),
        in_specs=[pl.BlockSpec(memory_space=pl.ANY)],
        out_specs=pl.BlockSpec(memory_space=pl.ANY),
        scratch_shapes=[dma(()), dma((Z - 1,)), dma((Z - 1,)), dma((n,)), dma((n,)), dma((m,)), dma((m,))],
        compiler_params=pltpu.CompilerParams(collective_id=0, has_side_effects=True, vmem_limit_bytes=56 << 20),
        cost_estimate=pl.CostEstimate(flops=0, bytes_accessed=20 * R * W * Z, transcendentals=0),
    )(x)


def join_kernel(*refs, count):
    t = pl.program_id(0)
    stacks, tail, out = refs[:-2], refs[-2], refs[-1]
    for i, ref in enumerate(stacks):
        @pl.when((t >= i * count) & (t < (i + 1) * count))
        def _(ref=ref):
            out[...] = ref[0]

    @pl.when(t >= len(stacks) * count)
    def _():
        out[:, :tail.shape[1]] = tail[...]


def join(stacks, tail):
    C, R, W = stacks[0].shape
    n = len(stacks)
    T = tail.shape[1]

    def at(i):
        return lambda t: (jnp.clip(t - i * C, 0, C - 1), 0, 0)
    return pl.pallas_call(functools.partial(join_kernel, count=C),
        out_shape=jax.ShapeDtypeStruct((R, n * C * W + T), bf16),
        grid=(n * C + 1,),
        in_specs=[pl.BlockSpec((1, R, W), at(i)) for i in range(n)] + [pl.BlockSpec((R, T), lambda t: (0, 0))],
        out_specs=pl.BlockSpec((R, W), lambda t: (0, t)),
        compiler_params=pltpu.CompilerParams(vmem_limit_bytes=56 << 20),
        cost_estimate=pl.CostEstimate(flops=0, bytes_accessed=4 * R * (n * C * W + T), transcendentals=0),
    )(*stacks, tail)


def deal_kernel(x_ref, o_ref):
    o_ref[0] = x_ref[...]


def deal(x, first, C, W):
    R = x.shape[0]
    return pl.pallas_call(deal_kernel,
        out_shape=jax.ShapeDtypeStruct((C, R, W), bf16),
        grid=(C,),
        in_specs=[pl.BlockSpec((R, W), lambda t: (0, first + t))],
        out_specs=pl.BlockSpec((1, R, W), lambda t: (t, 0, 0)),
        compiler_params=pltpu.CompilerParams(vmem_limit_bytes=56 << 20),
        cost_estimate=pl.CostEstimate(flops=0, bytes_accessed=4 * R * C * W, transcendentals=0),
    )(x)


def gather_kernel(x_ref, o_ref, own_sem, zs, zr, xs, xr, cs, cr, *, Z, C, quarter):
    z, a, c = lax.axis_index("zz"), lax.axis_index("core"), lax.axis_index("ctx")
    mesh_id = pl.DeviceIdType.MESH
    other = 1 - a
    peers = [(lax.rem(z + k, Z), a, c) for k in range(1, Z)] + [(z, a, lax.rem(c + j, C)) for j in range(1, C)] + [(z, other, c)]
    barrier = pltpu.get_barrier_semaphore()
    for peer in peers:
        pl.semaphore_signal(barrier, inc=1, device_id=peer, device_id_type=mesh_id)
    pl.semaphore_wait(barrier, len(peers))

    f = 2 * z + a

    def cols(q):
        return pl.ds(pl.multiple_of(q * quarter, quarter), quarter)

    def send(src, dst, s, r, peer):
        copy = pltpu.make_async_remote_copy(src_ref=src, dst_ref=dst, send_sem=s, recv_sem=r, device_id=peer, device_id_type=mesh_id)
        copy.start()
        return copy

    along = []
    for k in range(1, Z):
        along.append(send(x_ref.at[:, cols(c)], o_ref.at[f, :, cols(c)], zs.at[k - 1], zr.at[k - 1], peers[k - 1]))
    own = pltpu.make_async_copy(x_ref, o_ref.at[f], own_sem)
    own.start()
    whole = send(x_ref, o_ref.at[f], cs.at[0], cr.at[0], peers[-1])
    plane, cross = [], []
    for k in range(1, Z):
        along[k - 1].wait_recv()
        fs = 2 * lax.rem(z + Z - k, Z) + a
        piece = o_ref.at[fs, :, cols(c)]
        for j in range(1, C):
            n = (k - 1) * (C - 1) + j - 1
            plane.append(send(piece, piece, xs.at[n], xr.at[n], peers[Z - 1 + j - 1]))
        n = 1 + (k - 1) * C
        cross.append(send(piece, piece, cs.at[n], cr.at[n], peers[-1]))
    for k in range(1, Z):
        fs = 2 * lax.rem(z + Z - k, Z) + a
        for j in range(1, C):
            plane[(k - 1) * (C - 1) + j - 1].wait_recv()
            piece = o_ref.at[fs, :, cols(lax.rem(c + C - j, C))]
            n = 1 + (k - 1) * C + j
            cross.append(send(piece, piece, cs.at[n], cr.at[n], peers[-1]))
    for copy in along + plane:
        copy.wait_send()
    whole.wait_send()
    whole.wait_recv()
    for copy in cross:
        copy.wait_send()
        copy.wait_recv()
    own.wait()


def gather_all(x, Z, C):
    R, W = x.shape
    dma = pltpu.SemaphoreType.DMA
    n, m = (Z - 1) * (C - 1), 1 + (Z - 1) * C
    return pl.pallas_call(functools.partial(gather_kernel, Z=Z, C=C, quarter=W // C),
        out_shape=jax.ShapeDtypeStruct((2 * Z, R, W), bf16),
        in_specs=[pl.BlockSpec(memory_space=pl.ANY)],
        out_specs=pl.BlockSpec(memory_space=pl.ANY),
        scratch_shapes=[dma(()), dma((Z - 1,)), dma((Z - 1,)), dma((n,)), dma((n,)), dma((m,)), dma((m,))],
        compiler_params=pltpu.CompilerParams(collective_id=0, has_side_effects=True, vmem_limit_bytes=56 << 20),
        cost_estimate=pl.CostEstimate(flops=0, bytes_accessed=20 * R * W * Z, transcendentals=0),
    )(x)


HEADS = 17
EPSILON = 1e-05
FS = ("zz", "core")


def norm_parts(v):
    mean = jnp.mean(v, axis=-1, keepdims=True)
    c = v - mean
    r = lax.rsqrt(jnp.mean(c * c, axis=-1, keepdims=True) + EPSILON)
    return c * r, r


def norm_back(dn, v, gain):
    xhat, r = norm_parts(v)
    y = dn * gain
    a = jnp.mean(y, axis=-1, keepdims=True)
    b = jnp.mean(y * xhat, axis=-1, keepdims=True)
    return r * (y - a - xhat * b), jnp.sum(dn * xhat, axis=0), jnp.sum(dn, axis=0)


def col_sum(x):
    return jnp.dot(jnp.ones((16, x.shape[0]), bf16), x, preferred_element_type=f32)[0]


def gelu_parts(u):
    z = jnp.abs(u) * 0.7071067811865476
    t = 1.0 / (1.0 + 0.3275911 * z)
    e = jnp.exp(-z * z)
    poly = t * (0.254829592 + t * (-0.284496736 + t * (1.421413741 + t * (-1.453152027 + t * 1.061405429))))
    half = 0.5 * poly * e
    cdf = jnp.where(u >= 0, 1.0 - half, half)
    return u * cdf, cdf + u * e * 0.3989422804014327


def local(
    tokens, cotangent, lengths, block_order,
    ln1_gain, ln1_bias, qkv_weight, q_bias, v_bias, out_weight, out_bias,
    ln2_gain, ln2_bias, up_weight, up_bias, down_weight, down_bias,
    *, G, S,
):
    slots, rows, width = tokens.shape
    C = lax.axis_size("ctx")
    me = lax.axis_index("ctx")
    N = rows * C
    B = rows // 2
    NB = 2 * C
    L = ln1_gain.shape[0]
    shard = ln1_gain.shape[1]
    HW = G * 128
    x_tokens = tokens[0]

    steps = jnp.arange(NB, dtype=jnp.int32)
    order = block_order[0]
    inverse = jnp.sum(jnp.where(order[None, :] == steps[:, None], steps[None, :], 0), axis=1).astype(jnp.int32)
    count = (lengths + (B - 1)) // B
    meta = jnp.concatenate([inverse, count])
    def swap(x):
        return lax.ppermute(x, "core", [(0, 1), (1, 0)])

    metas = [meta, swap(meta)][:S]
    phase_inv = [t[None, :NB] for t in metas]
    phase_nb = [t[NB:] for t in metas]
    own = jnp.concatenate([inverse, lax.dynamic_slice_in_dim(order, 2 * me, 2, 0), count])
    own_pos = (lax.dynamic_slice_in_dim(order, 2 * me, 2, 0)[:, None] * B + jnp.arange(B, dtype=jnp.int32)).reshape(rows, 1)
    live = (own_pos < lengths[0]).astype(f32)

    def pack(w):
        parts = []
        for g in range(G):
            parts += [w[:, kind * width + g * 128:kind * width + g * 128 + 128] for kind in range(3)]
        last = width - 64
        parts += [w[:, kind * width + last:kind * width + width] for kind in (1, 2, 0)]
        return jnp.concatenate(parts, axis=1)

    def unpack(w):
        tail = G * 384
        parts = []
        for kind, last in enumerate((128, 0, 64)):
            parts += [w[:, g * 384 + kind * 128:g * 384 + kind * 128 + 128] for g in range(G)]
            parts.append(w[:, tail + last:tail + last + 64])
        return jnp.concatenate(parts, axis=1)

    def fetch(w):
        return lax.all_gather(w.astype(bf16), FS, axis=0, tiled=True)

    vectors = [ln1_gain, ln1_bias, q_bias, v_bias, out_bias, ln2_gain, ln2_bias, down_bias]
    vec = [t.astype(bf16).T for t in vectors] + [up_bias.astype(bf16).reshape(4 * L, shard).T]
    first = pack(qkv_weight[0].astype(bf16))
    block = jnp.concatenate([first] + vec, axis=1)
    used = block.shape[1]
    if C == 4 and lax.axis_size("zz") == 4:
        block = jnp.pad(block, ((0, 0), (0, -used % (128 * C))))
        block = gather_all(block, 4, C)
    else:
        block = lax.all_gather(block, FS)
    first_w = block[:, :, :3 * width].reshape(width, 3 * width)
    vec = jnp.transpose(block[:, :, 3 * width:used].reshape(width, used - 3 * width)).astype(f32)

    def vector(index, layer):
        if index < 8:
            return vec[L * index + layer]
        t = vec[8 * L + 4 * layer:8 * L + 4 * layer + 4]
        return jnp.transpose(t.reshape(4, -1, shard), (1, 0, 2)).reshape(-1)

    weights = []
    for layer in range(L):
        weights.append((
            fetch(pack(qkv_weight[layer].astype(bf16))) if layer else first_w,
            fetch(out_weight[layer]),
            fetch(up_weight[layer]),
            fetch(down_weight[layer]),
        ))

    def plain(x):
        return with_layout_constraint(x, Layout(major_to_minor=tuple(range(x.ndim))))

    def exchange(x):
        return plain(lax.all_to_all(plain(x), "ctx", 0, 0))

    def after(x, *others):
        return lax.optimization_barrier((x,) + others)

    stream = x_tokens.astype(f32)
    records = []
    for layer in range(L):
        qkv_w, out_w, up_w, down_w = weights[layer]
        xhat, _ = norm_parts(stream)
        n1 = (xhat * vector(0, layer) + vector(1, layer)).astype(bf16)
        q_b, v_b = vector(2, layer), vector(3, layer)
        bias = pack(jnp.concatenate([q_b, jnp.zeros_like(q_b), v_b])[None])[0]
        projected = (jnp.dot(n1, qkv_w, preferred_element_type=f32) + bias).astype(bf16)
        wide = [deal(projected, s * C, C, 384) for s in range(S)]
        tail = projected[:, G * 384:]
        if S == 2:
            wide[1] = swap(wide[1])
        kv16 = jnp.broadcast_to(tail[None, :, :128], (C, rows, 128))
        q16 = tail[:, 128:]
        heads, o, lse, o_back = [], [], [], []
        for s in range(S):
            t = wide[s]
            if s == S - 1:
                t = jnp.concatenate([t, kv16], axis=2)
            if s:
                t, heads[0] = after(t, heads[0])
            heads.append(exchange(t).reshape(1, N, -1))
        for s in range(S):
            o_s, lse_s = flash_fwd(heads[s], phase_inv[s], phase_nb[s], B)
            o.append(o_s)
            lse.append(lse_s)
            t = o_s.reshape(C, rows, 128)
            if s:
                t, o_back[0] = after(t, o_back[0])
            o_back.append(exchange(swap(t) if s else t))
        o16, lse16 = one_fwd(q16, heads[-1][0], own, B)
        mixed = join(o_back, o16)
        m = stream + jnp.dot(mixed, out_w, preferred_element_type=f32) + vector(4, layer)
        xhat2, _ = norm_parts(m)
        n2 = (xhat2 * vector(5, layer) + vector(6, layer)).astype(bf16)
        u = jnp.dot(n2, up_w, preferred_element_type=f32) + vector(8, layer)
        a, slope = gelu_parts(u)
        a = a.astype(bf16)
        a, slope = after(a, slope.astype(bf16))
        records.append((stream, n1, heads, q16, o, lse, o16, lse16, mixed, m, n2, a, slope))
        if layer < L - 1:
            stream = m + jnp.dot(a, down_w, preferred_element_type=f32) + vector(7, layer)
    end_a, end_m, end_w, end_b = a, m, down_w, vector(7, L - 1)

    def reduce_fsdp(g):
        return lax.psum_scatter(g.astype(bf16), FS, scatter_dimension=0, tiled=True)

    def reduce_ctx(g):
        return lax.psum(g, "ctx").astype(f32)

    grad = cotangent[0].astype(f32) * live
    matrices = [None] * L
    fours = [None] * L
    ffns = [None] * L
    small = [None] * L

    def ctx_end(mine):
        return exchange(jnp.broadcast_to(mine[None], (C,) + mine.shape))

    def ctx_sum(shards):
        mine, sizes = ctx_begin(shards)
        return ctx_end(mine), sizes

    def ctx_begin(shards):
        pieces = []
        for t in shards:
            if t.shape[1] == width:
                pieces.append(t.reshape(C, -1, width))
            else:
                pieces.append(jnp.transpose(t.reshape(t.shape[0], C, -1), (1, 0, 2)).reshape(C, -1, width))
        sizes = [t.shape[1] for t in pieces]
        parts = exchange(jnp.concatenate(pieces, axis=1))
        mine = jnp.sum(parts.astype(f32), axis=0).astype(bf16)
        return mine, sizes

    def spread(summed, shapes):
        whole, sizes = summed
        out, at = [], 0
        for n, (r, c) in zip(sizes, shapes):
            t = whole[:, at:at + n].astype(f32)
            at += n
            if c == width:
                out.append(t.reshape(r, c))
            else:
                out.append(jnp.transpose(t.reshape(C, r, c // C), (1, 0, 2)).reshape(r, c))
        return out

    wide_shape, tall_shape = (shard, 4 * width), (4 * shard, width)
    for layer in reversed(range(L)):
        stream_in, n1, heads, q16, o, lse, o16, lse16, mixed, m, n2, a, slope = records[layer]
        qkv_w, out_w, up_w, down_w = weights[layer]
        gb = grad.astype(bf16)
        d_down_b = col_sum(gb)
        d_down = jnp.einsum("rf,rd->fd", a, gb, preferred_element_type=f32).astype(bf16)
        gb, d_down = after(gb, plain(d_down))
        if layer < L - 1:
            above = list(after(gb, *ffns[layer + 1]))
            gb = above.pop(0)
            mine_ffn, ffn_sizes = ctx_begin(above)
        d_down = reduce_fsdp(d_down)
        du = (jnp.einsum("rd,fd->rf", gb, down_w, preferred_element_type=f32) * slope.astype(f32)).astype(bf16)
        d_up_b = col_sum(du)
        if layer < L - 1:
            du, mine_ffn = after(du, mine_ffn)
            ffn_whole = ctx_end(mine_ffn)
        d_up = jnp.einsum("rd,rf->df", n2, du, preferred_element_type=f32).astype(bf16)
        du, d_up = after(du, plain(d_up))
        d_up = reduce_fsdp(d_up)
        dn2 = jnp.einsum("rf,df->rd", du, up_w, preferred_element_type=f32)
        back, d_gain2, d_bias2 = norm_back(dn2, m, vector(5, layer))
        gm = grad + back
        gmb = gm.astype(bf16)
        d_out_b = col_sum(gmb)
        d_out = jnp.einsum("rd,re->de", mixed, gmb, preferred_element_type=f32).astype(bf16)
        if layer == 0:
            gmb, d_out = after(gmb, plain(d_out))
        if layer < L - 1:
            gmb, ffn_whole = after(gmb, ffn_whole)
        d_o = []
        for s in range(S):
            w = out_w[C * 128 * s:C * 128 * (s + 1)].reshape(C, 128, width)
            d_o.append(jnp.einsum("re,gce->grc", gmb, w, preferred_element_type=f32).astype(bf16))
        d_o16 = jnp.einsum("re,ce->rc", gmb, out_w[HW:], preferred_element_type=f32).astype(bf16)
        dq16, dkv16 = one_bwd(q16, heads[-1][0], o16, d_o16, lse16, own, B)
        d_oh, d_wide = [], []
        for s in range(S):
            t = d_o[s]
            if s:
                t = swap(t)
            if s == S - 1:
                t = jnp.concatenate([t, dkv16.reshape(C, rows, 128)], axis=2)
            if s:
                t, d_oh[0] = after(t, d_oh[0])
            if s == S - 1 and layer < L - 1:
                t, fours[layer + 1] = after(t, fours[layer + 1])
            d_oh.append(exchange(t).reshape(1, N, -1))
        dkv16 = jnp.sum(d_oh[-1].reshape(C, rows, 256)[:, :, 128:].astype(f32), axis=0)
        for s in range(S):
            t = flash_bwd(heads[s], o[s], d_oh[s], lse[s], phase_inv[s], phase_nb[s], B)
            t = t.reshape(C, rows, 384)
            if s:
                t, d_wide[0] = after(t, d_wide[0])
            if s == S - 1:
                t, d_down = after(t, d_down)
            if s == S - 1 and layer:
                t, d_up = after(t, d_up)
            d_wide.append(exchange(swap(t) if s else t))
        d_tail = jnp.concatenate([dkv16.astype(bf16), dq16], axis=1)
        d_row = join(d_wide, d_tail)
        d_row, d_down_b, d_up_b, d_out_b = after(d_row, d_down_b, d_up_b, d_out_b)
        d_back = d_row
        if layer == 0:
            d_row, d_up = after(d_row, d_up)
            mine, middle_sizes = ctx_begin([fours[1], d_up, d_down])
            d_back, mine = after(d_row, mine)
        d_qkv = jnp.einsum("rd,rc->dc", n1, d_row, preferred_element_type=f32).astype(bf16)
        if layer:
            d_row, d_four = after(d_row, plain(jnp.concatenate([d_qkv, d_out], axis=1)))
            d_four = reduce_fsdp(d_four)
        else:
            d_qkv, d_out = after(d_qkv, reduce_fsdp(d_out))
            d_four = jnp.concatenate([reduce_fsdp(d_qkv), d_out], axis=1)
        sums = unpack(col_sum(d_row)[None])[0]
        dn1 = jnp.einsum("rc,dc->rd", d_back, qkv_w, preferred_element_type=f32)
        back, d_gain1, d_bias1 = norm_back(dn1, stream_in, vector(0, layer))
        grad = gm + back
        fours[layer] = d_four
        ffns[layer] = (d_up, d_down)
        small[layer] = jnp.concatenate([
            t.reshape(-1, n) for t, n in (
                (d_gain1, shard), (d_bias1, shard), (sums[:width], shard), (sums[2 * width:], shard), (d_out_b, shard),
                (d_gain2, shard), (d_bias2, shard), (d_down_b, shard), (d_up_b, 4 * shard))], axis=1)

    vec_grads = jnp.stack(small, axis=1)
    vec_grads = jnp.sum(lax.all_to_all(vec_grads, FS, 0, 0), axis=0)
    vec_grads = jnp.sum(lax.all_to_all(jnp.broadcast_to(vec_grads[None], (C,) + vec_grads.shape), "ctx", 0, 0), axis=0)
    end, vec_grads = after(fours[0], vec_grads)
    mine_last, last_sizes = ctx_begin([end])
    end_a, mine_last = after(end_a, mine_last)
    whole = ctx_end(jnp.concatenate([mine, mine_last], axis=0))
    stream = end_m + jnp.dot(end_a, end_w, preferred_element_type=f32) + end_b
    activations = (stream * live).astype(bf16)[None]
    activations, whole = after(activations, whole)
    rest = spread((whole, middle_sizes + last_sizes), [wide_shape, wide_shape, tall_shape, wide_shape])
    matrices[1] = [rest[0]] + spread((ffn_whole, ffn_sizes), [wide_shape, tall_shape])
    matrices[0] = [rest[3], rest[1], rest[2]]
    vg = [vec_grads[:, i * shard:(i + 1) * shard] for i in range(8)] + [vec_grads[:, 8 * shard:]]

    g_qkv = jnp.stack([unpack(matrices[layer][0][:, :3 * width]) for layer in range(L)])
    g_out = jnp.stack([matrices[layer][0][:, 3 * width:] for layer in range(L)])
    g_up = jnp.stack([matrices[layer][1] for layer in range(L)])
    g_down = jnp.stack([matrices[layer][2] for layer in range(L)])
    return (activations, grad[None], vg[0], vg[1], g_qkv, vg[2], vg[3], g_out, vg[4], vg[5], vg[6], g_up, vg[8], g_down, vg[7])


def solution(mesh):
    F, C = mesh.devices.shape
    inner = Mesh(mesh.devices.reshape(F // 2, 2, C), ("zz", "core", "ctx"))
    S = 2 if 16 // (2 * C) >= 2 else 1
    G = S * C
    rows = P(FS, "ctx", None)
    vec, mat = P(None, FS), P(None, FS, None)
    return jax.shard_map(
        functools.partial(local, G=G, S=S),
        mesh=inner,
        in_specs=(rows, rows, P(FS), P(FS, None), vec, vec, mat, vec, vec, mat, vec, vec, vec, mat, vec, mat, vec),
        out_specs=(rows, rows, vec, vec, mat, vec, vec, mat, vec, vec, vec, mat, vec, mat, vec),
        check_vma=False,
    )
```

profile of v0, /device:TPU:0, one launch (start us, length us, event | category | flops | bytes accessed | tf_op | source)
XLA Modules:
  0.0 1501.8 jit_solution(9556707588138426853)
XLA Ops:
  30.9 54.5 %shard_map.280 = bf16[8,136,3584]{2,1,0:T(8,128)(2,1)} custom-call(bf16[136,3584]{1,0:T(8,128)(2,1)} %pad.4.x_ref), custom_call_target="tpu_custom_call" | custom-call | bytes 38993920 | tf_op jit(solution)/shard_map/pallas_call | solution.py:512
  128.3 31.4 %all-to-all-done = bf16[4,1024,384]{2,1,0:T(8,128)(2,1)S(1)} async-done(((bf16[4,1024,384]{2,1,0:T(8,128)(2,1)}), bf16[4,1024,384]{2,1,0:T(8,128)(2,1)S(1)}, u32[]{:S(2)}, u32[]{:S(2)}) %all-to-all-start) | async-done | bytes 3145760 | tf_op jit(solution)/shard_map/all_to_all | solution.py:639
  173.9 38.1 %all-to-all-done.1 = bf16[4,1024,512]{2,1,0:T(8,128)(2,1)} async-done(((bf16[4,1024,512]{2,1,0:T(8,128)(2,1)}), bf16[4,1024,512]{2,1,0:T(8,128)(2,1)}, u32[]{:S(2)}, u32[]{:S(2)}) %all-to-all-start.1) | async-done | bytes 4194336 | tf_op jit(solution)/shard_map/all_to_all | solution.py:639
  265.1 36.2 %add_convert_fusion.1 = (bf16[1024,4352]{1,0:T(8,128)(2,1)}, bf16[1024,4352]{1,0:T(8,128)(2,1)}) fusion(f32[4352]{0:T(1024)S(1)} %add.281, bf16[1,1088,4352]{2,1,0:T(8,128)(2,1)} %all-gather.18.cloned.1.call-done, f32[1024,1088]{0,1:T(8,128)} %copy-done.50, f32[1088]{0:T(1024)S(1)} %copy-done.105, f32[1088]{0:T(1024)S(1)} %get-tuple-element.207, ...), kind=kOutput, calls=%fused_computation.14 | convolution fusion | flops 9827581952 | bytes 31786496 | tf_op jit(solution)/shard_map/dot_general | solution.py:680
  301.3 17.8 %fusion.157 = (f32[1024]{0:T(1024)S(1)}, f32[1024,1088]{0,1:T(8,128)}) fusion(f32[1088]{0:T(1024)S(1)} %copy-done.111, f32[1024,1088]{0,1:T(8,128)} %copy-done.50, bf16[1024,4352]{1,0:T(8,128)(2,1)} %get-tuple-element.105, bf16[1,4352,1088]{2,1,0:T(8,128)(2,1)} %all-gather.20.cloned.1.call-done), kind=kOutput, calls=%fused_computation.290 | convolution fusion | flops 9700572160 | bytes 27304192 | tf_op jit(solution)/shard_map/dot_general | solution.py:686
  355.6 30.8 %all-to-all-done.4 = bf16[4,1024,384]{2,1,0:T(8,128)(2,1)S(1)} async-done(((bf16[4,1024,384]{2,1,0:T(8,128)(2,1)}), bf16[4,1024,384]{2,1,0:T(8,128)(2,1)S(1)}, u32[]{:S(2)}, u32[]{:S(2)}) %all-to-all-start.4) | async-done | bytes 3145760 | tf_op jit(solution)/shard_map/all_to_all | solution.py:639
  397.4 41.5 %all-to-all-done.5 = bf16[4,1024,512]{2,1,0:T(8,128)(2,1)} async-done(((bf16[4,1024,512]{2,1,0:T(8,128)(2,1)}), bf16[4,1024,512]{2,1,0:T(8,128)(2,1)}, u32[]{:S(2)}, u32[]{:S(2)}) %all-to-all-start.5) | async-done | bytes 4194336 | tf_op jit(solution)/shard_map/all_to_all | solution.py:639
  493.2 36.5 %add_convert_fusion = (bf16[1024,4352]{1,0:T(8,128)(2,1)}, bf16[1024,4352]{1,0:T(8,128)(2,1)}) fusion(f32[4352]{0:T(1024)S(1)} %add.309, bf16[1,1088,4352]{2,1,0:T(8,128)(2,1)} %all-gather.24.cloned.1.call-done, f32[1024,1088]{0,1:T(8,128)} %copy-done.39, f32[1088]{0:T(1024)S(1)} %copy-done.109, f32[1088]{0:T(1024)S(1)} %copy-done.70, ...), kind=kOutput, calls=%fused_computation.12 | convolution fusion | flops 9827581952 | bytes 31786496 | tf_op jit(solution)/shard_map/dot_general | solution.py:680
  529.7 17.6 %convolution_convert_fusion.3 = bf16[4352,1088]{1,0:T(8,128)(2,1)} fusion(bf16[1024,4352]{1,0:T(8,128)(2,1)} %get-tuple-element.174, bf16[1024,1088]{0,1:T(8,128)(2,1)S(1)} %copy-done.53), kind=kOutput, calls=%fused_computation.7 | convolution fusion | flops 9701965824 | bytes 20611072 | tf_op jit(solution)/shard_map/rf,rd->fd/dot_general | solution.py:738
  547.4 19.8 %multiply_convert_fusion.1 = bf16[1024,4352]{1,0:T(8,128)(2,1)} fusion(bf16[1024,4352]{1,0:T(8,128)(2,1)} %get-tuple-element.115, bf16[1024,1088]{0,1:T(8,128)(2,1)} %fusion.55, bf16[1,4352,1088]{2,1,0:T(8,128)(2,1)} %all-gather.26.cloned.1.call-done), kind=kOutput, calls=%fused_computation.11 | convolution fusion | flops 9710600192 | bytes 29523968 | tf_op jit(solution)/shard_map/rd,fd->rf/dot_general | solution.py:745
  586.2 19.2 %multiply_reduce_fusion = (f32[1088]{0:T(1024)}, f32[1024]{0:T(1024)S(1)}, f32[1024]{0:T(1024)S(1)}, f32[1088]{0:T(1024)}, f32[1024,1088]{0,1:T(8,128)S(1)}) fusion(f32[1024,1088]{0,1:T(8,128)} %copy-done.39, f32[1024]{0:T(1024)S(1)} %add_rsqrt_fusion, f32[1024]{0:T(1024)S(1)} %broadcast_multiply_fusion.8, f32[1088]{0:T(1024)S(1)} %copy-done.70, ...), kind=kOutput, calls=%fused_computation.72 | convolution fusion | flops 9707253760 | bytes 27325184 | tf_op jit(solution)/shard_map/rf,df->rd/dot_general | solution.py:753
  682.0 19.0 %all-to-all-done.10.refs_0_ = bf16[4,1024,384]{2,1,0:T(8,128)(2,1)} async-done(((bf16[4,1024,384]{2,1,0:T(8,128)(2,1)}), bf16[4,1024,384]{2,1,0:T(8,128)(2,1)}, u32[]{:S(2)}, u32[]{:S(2)}) %all-to-all-start.10) | async-done | bytes 3145760 | tf_op jit(solution)/shard_map/all_to_all | solution.py:639
  701.0 20.3 %reduce-scatter.10.cloned.1.call-done = bf16[544,1088]{1,0:T(8,128)(2,1)} async-done(((bf16[4352,1088]{1,0:T(8,128)(2,1)}), bf16[544,1088]{1,0:T(8,128)(2,1)}) %reduce-scatter.10.cloned.1.call-update) | async-done | bytes 1183760 | tf_op jit(solution)/shard_map/reduce_scatter | solution.py:690
  721.3 100.8 %reduce-scatter.12.cloned.1.call-done = bf16[136,4352]{1,0:T(8,128)(2,1)} async-done(((bf16[1088,4352]{1,0:T(8,128)(2,1)}), bf16[136,4352]{1,0:T(8,128)(2,1)}) %reduce-scatter.12.cloned.1.call-update) | async-done | bytes 1183760 | tf_op jit(solution)/shard_map/reduce_scatter | solution.py:690
  850.4 19.1 %all-to-all-done.11.refs_1_ = bf16[4,1024,384]{2,1,0:T(8,128)(2,1)} async-done(((bf16[4,1024,384]{2,1,0:T(8,128)(2,1)}), bf16[4,1024,384]{2,1,0:T(8,128)(2,1)}, u32[]{:S(2)}, u32[]{:S(2)}) %all-to-all-start.11) | async-done | bytes 3145760 | tf_op jit(solution)/shard_map/all_to_all | solution.py:639
  945.3 19.8 %multiply_convert_fusion = bf16[1024,4352]{1,0:T(8,128)(2,1)} fusion(bf16[1024,4352]{1,0:T(8,128)(2,1)} %get-tuple-element.135, bf16[1024,1088]{0,1:T(8,128)(2,1)} %copy-done.52, bf16[1,4352,1088]{2,1,0:T(8,128)(2,1)} %all-gather.20.cloned.1.call-done), kind=kOutput, calls=%fused_computation.10 | convolution fusion | flops 9710600192 | bytes 29523968 | tf_op jit(solution)/shard_map/rd,fd->rf/dot_general | solution.py:745
  1001.7 19.9 %multiply_reduce_fusion.2 = (f32[1088]{0:T(1024)}, f32[1024]{0:T(1024)S(1)}, f32[1024]{0:T(1024)S(1)}, f32[1088]{0:T(1024)}, f32[1024,1088]{0,1:T(8,128)S(1)}) fusion(f32[1024,1088]{0,1:T(8,128)} %copy-done.50, f32[1024]{0:T(1024)S(1)} %copy-done.101, f32[1024]{0:T(1024)S(1)} %copy-done.79, f32[1088]{0:T(1024)S(1)} %copy-done.85, ...), kind=kOutput, calls=%fused_computation.74 | convolution fusion | flops 9707253760 | bytes 27325184 | tf_op jit(solution)/shard_map/rf,df->rd/dot_general | solution.py:753
  1107.6 19.9 %all-to-all-done.16.refs_0_ = bf16[4,1024,384]{2,1,0:T(8,128)(2,1)} async-done(((bf16[4,1024,384]{2,1,0:T(8,128)(2,1)}), bf16[4,1024,384]{2,1,0:T(8,128)(2,1)}, u32[]{:S(2)}, u32[]{:S(2)}) %all-to-all-start.16) | async-done | bytes 3145760 | tf_op jit(solution)/shard_map/all_to_all | solution.py:639
  1147.6 27.3 %all-to-all-done.17.refs_1_ = bf16[4,1024,384]{2,1,0:T(8,128)(2,1)} async-done(((bf16[4,1024,384]{2,1,0:T(8,128)(2,1)}), bf16[4,1024,384]{2,1,0:T(8,128)(2,1)}, u32[]{:S(2)}, u32[]{:S(2)}) %all-to-all-start.17) | async-done | bytes 3145760 | tf_op jit(solution)/shard_map/all_to_all | solution.py:639
  1183.8 21.7 %reduce-scatter.18.cloned.1.call-done = bf16[136,4352]{1,0:T(8,128)(2,1)} async-done(((bf16[1088,4352]{1,0:T(8,128)(2,1)}), bf16[136,4352]{1,0:T(8,128)(2,1)}) %reduce-scatter.18.cloned.1.call-update) | async-done | bytes 1183760 | tf_op jit(solution)/shard_map/reduce_scatter | solution.py:690
  1218.6 26.5 %reduce-scatter.22.cloned.1.call-done = bf16[136,1088]{1,0:T(8,128)(2,1)} async-done(((bf16[1088,1088]{1,0:T(8,128)(2,1)}), bf16[136,1088]{1,0:T(8,128)(2,1)}) %reduce-scatter.22.cloned.1.call-update) | async-done | bytes 295952 | tf_op jit(solution)/shard_map/optimization_barrier | solution.py:642
  1279.2 34.0 %all-to-all-done.18 = bf16[4,408,1088]{2,1,0:T(8,128)(2,1)} async-done(((bf16[4,408,1088]{2,1,0:T(8,128)(2,1)}), bf16[4,408,1088]{2,1,0:T(8,128)(2,1)}, u32[]{:S(2)}, u32[]{:S(2)}) %all-to-all-start.18) | async-done | bytes 3551264 | tf_op jit(solution)/shard_map/all_to_all | solution.py:639
  1332.2 21.6 %all_to_all.115 = f32[8,2,1632]{2,1,0:T(2,128)S(1)} all-to-all(f32[8,2,1632]{2,1,0:T(2,128)S(1)} %pad_maximum_fusion.13), channel_id=1, replica_groups=mesh['zz'=4,'core'=2,'ctx'=4] {'zz','core'}, dimensions={0} | all-to-all | bytes 208896 | tf_op jit(solution)/shard_map/all_to_all | solution.py:819
  1423.5 29.8 %all-to-all-done.22 = bf16[4,544,1088]{2,1,0:T(8,128)(2,1)} async-done(((bf16[4,544,1088]{2,1,0:T(8,128)(2,1)}), bf16[4,544,1088]{2,1,0:T(8,128)(2,1)}, u32[]{:S(2)}, u32[]{:S(2)}) %all-to-all-start.22) | async-done | bytes 4735008 | tf_op jit(solution)/shard_map/all_to_all | solution.py:639
  (621 shorter events, 761.4 us)
Async XLA Ops:
  7.2 249.0 %all-gather.16.cloned.1.call-start = ((), (), s32[]{:S(2)}) async-start(), calls=%async_computation.37 | async-start | bytes 2820096 | tf_op jit(solution)/shard_map/all_gather | solution.py:605
  9.5 255.5 %all-gather.18.cloned.1.call-start = ((), (), s32[]{:S(2)}) async-start(), calls=%async_computation.38 | async-start | bytes 10653696 | tf_op jit(solution)/shard_map/all_gather | solution.py:605
  13.7 287.6 %all-gather.20.cloned.1.call-start = ((), (), s32[]{:S(2)}) async-start(), calls=%async_computation.39 | async-start | bytes 11280384 | tf_op jit(solution)/shard_map/all_gather | solution.py:605
  18.1 303.8 %all-gather.14.cloned.1.call-start = ((), (), s32[]{:S(2)}) async-start(), calls=%async_computation.30 | async-start | bytes 8146944 | tf_op jit(solution)/shard_map/all_gather | solution.py:605
  119.3 40.5 %all-to-all-start = ((bf16[4,1024,384]{2,1,0:T(8,128)(2,1)}), bf16[4,1024,384]{2,1,0:T(8,128)(2,1)S(1)}, u32[]{:S(2)}, u32[]{:S(2)}) async-start(bf16[4,1024,384]{2,1,0:T(8,128)(2,1)} %shard_map.282), calls=%async_computation | async-start | bytes 6291456 | tf_op jit(solution)/shard_map/all_to_all | solution.py:639
  123.2 360.1 %all-gather.22.cloned.1.call-start = ((), (), s32[]{:S(2)}) async-start(), calls=%async_computation.40 | async-start | bytes 2820096 | tf_op jit(solution)/shard_map/all_gather | solution.py:605
  159.8 52.2 %all-to-all-start.1 = ((bf16[4,1024,512]{2,1,0:T(8,128)(2,1)}), bf16[4,1024,512]{2,1,0:T(8,128)(2,1)}, u32[]{:S(2)}, u32[]{:S(2)}) async-start(bf16[4,1024,512]{2,1,0:T(8,128)(2,1)} %pad_maximum_fusion.1), calls=%async_computation.1 | async-start | bytes 8388608 | tf_op jit(solution)/shard_map/all_to_all | solution.py:639
  164.7 328.4 %all-gather.24.cloned.1.call-start = ((), (), s32[]{:S(2)}) async-start(), calls=%async_computation.41 | async-start | bytes 10653696 | tf_op jit(solution)/shard_map/all_gather | solution.py:605
  345.6 40.7 %all-to-all-start.4 = ((bf16[4,1024,384]{2,1,0:T(8,128)(2,1)}), bf16[4,1024,384]{2,1,0:T(8,128)(2,1)S(1)}, u32[]{:S(2)}, u32[]{:S(2)}) async-start(bf16[4,1024,384]{2,1,0:T(8,128)(2,1)} %shard_map.288), calls=%async_computation.4 | async-start | bytes 6291456 | tf_op jit(solution)/shard_map/all_to_all | solution.py:639
  349.3 198.1 %all-gather.26.cloned.1.call-start = ((), (), s32[]{:S(2)}) async-start(), calls=%async_computation.42 | async-start | bytes 11280384 | tf_op jit(solution)/shard_map/all_gather | solution.py:605
  386.4 52.6 %all-to-all-start.5 = ((bf16[4,1024,512]{2,1,0:T(8,128)(2,1)}), bf16[4,1024,512]{2,1,0:T(8,128)(2,1)}, u32[]{:S(2)}, u32[]{:S(2)}) async-start(bf16[4,1024,512]{2,1,0:T(8,128)(2,1)} %pad_maximum_fusion.2), calls=%async_computation.5 | async-start | bytes 8388608 | tf_op jit(solution)/shard_map/all_to_all | solution.py:639
  462.7 258.6 %reduce-scatter.10.cloned.1.call-start = ((), (), s32[]{:S(2)}) async-start(), calls=%async_computation.31 | async-start | bytes 11280384 | tf_op jit(solution)/shard_map/reduce_scatter | solution.py:690
  547.3 274.8 %reduce-scatter.12.cloned.1.call-start = ((), (), s32[]{:S(2)}) async-start(), calls=%async_computation.32 | async-start | bytes 10653696 | tf_op jit(solution)/shard_map/reduce_scatter | solution.py:690
  660.6 40.4 %all-to-all-start.10 = ((bf16[4,1024,384]{2,1,0:T(8,128)(2,1)}), bf16[4,1024,384]{2,1,0:T(8,128)(2,1)}, u32[]{:S(2)}, u32[]{:S(2)}) async-start(bf16[4,1024,384]{2,1,0:T(8,128)(2,1)} %bitcast.287), calls=%async_computation.10 | async-start | bytes 6291456 | tf_op jit(solution)/shard_map/all_to_all | solution.py:639
  828.1 41.4 %all-to-all-start.11 = ((bf16[4,1024,384]{2,1,0:T(8,128)(2,1)}), bf16[4,1024,384]{2,1,0:T(8,128)(2,1)}, u32[]{:S(2)}, u32[]{:S(2)}) async-start(bf16[4,1024,384]{2,1,0:T(8,128)(2,1)} %collective-permute-done.6), calls=%async_computation.13 | async-start | bytes 6291456 | tf_op jit(solution)/shard_map/all_to_all | solution.py:639
  832.7 226.0 %reduce-scatter.14.cloned.1.call-start = ((), (), s32[]{:S(2)}) async-start(), calls=%async_computation.33 | async-start | bytes 10653696 | tf_op jit(solution)/shard_map/reduce_scatter | solution.py:690
  896.7 230.8 %reduce-scatter.16.cloned.1.call-start = ((), (), s32[]{:S(2)}) async-start(), calls=%async_computation.34 | async-start | bytes 11280384 | tf_op jit(solution)/shard_map/reduce_scatter | solution.py:690
  945.0 260.4 %reduce-scatter.18.cloned.1.call-start = ((), (), s32[]{:S(2)}) async-start(), calls=%async_computation.35 | async-start | bytes 10653696 | tf_op jit(solution)/shard_map/reduce_scatter | solution.py:690
  1087.1 40.4 %all-to-all-start.16 = ((bf16[4,1024,384]{2,1,0:T(8,128)(2,1)}), bf16[4,1024,384]{2,1,0:T(8,128)(2,1)}, u32[]{:S(2)}, u32[]{:S(2)}) async-start(bf16[4,1024,384]{2,1,0:T(8,128)(2,1)} %bitcast.286), calls=%async_computation.19 | async-start | bytes 6291456 | tf_op jit(solution)/shard_map/all_to_all | solution.py:639
  1091.8 153.3 %reduce-scatter.22.cloned.1.call-start = ((), (), s32[]{:S(2)}) async-start(), calls=%async_computation.43 | async-start | bytes 2820096
  1133.5 41.4 %all-to-all-start.17 = ((bf16[4,1024,384]{2,1,0:T(8,128)(2,1)}), bf16[4,1024,384]{2,1,0:T(8,128)(2,1)}, u32[]{:S(2)}, u32[]{:S(2)}) async-start(bf16[4,1024,384]{2,1,0:T(8,128)(2,1)} %collective-permute-done.8), calls=%async_computation.21 | async-start | bytes 6291456 | tf_op jit(solution)/shard_map/all_to_all | solution.py:639
  1138.2 223.1 %reduce-scatter.20.cloned.1.call-start = ((), (), s32[]{:S(2)}) async-start(), calls=%async_computation.36 | async-start | bytes 8146944 | tf_op jit(solution)/shard_map/reduce_scatter | solution.py:690
  1267.8 45.4 %all-to-all-start.18 = ((bf16[4,408,1088]{2,1,0:T(8,128)(2,1)}), bf16[4,408,1088]{2,1,0:T(8,128)(2,1)}, u32[]{:S(2)}, u32[]{:S(2)}) async-start(bf16[4,408,1088]{2,1,0:T(8,128)(2,1)} %pad_maximum_fusion.3), calls=%async_computation.24 | async-start | bytes 7520256 | tf_op jit(solution)/shard_map/all_to_all | solution.py:639
  1392.4 60.8 %all-to-all-start.22 = ((bf16[4,544,1088]{2,1,0:T(8,128)(2,1)}), bf16[4,544,1088]{2,1,0:T(8,128)(2,1)}, u32[]{:S(2)}, u32[]{:S(2)}) async-start(bf16[4,544,1088]{2,1,0:T(8,128)(2,1)} %broadcast_in_dim.45), calls=%async_computation.28 | async-start | bytes 10027008 | tf_op jit(solution)/shard_map/all_to_all | solution.py:639
  (159 other events, 3244.7 us)
Sparse Core Ops, SparseCore 0:
  9.7 48.8 all-gather.15
  60.8 89.6 all-gather.17
  152.7 94.0 all-gather.19
  248.9 70.9 all-gather.13
  321.4 31.4 all-gather.21
  354.4 90.0 all-gather.23
  446.7 94.0 all-gather.25
  547.4 173.8 reduce-scatter.9
  723.6 98.4 reduce-scatter.11
  896.8 102.1 reduce-scatter.13
  1001.3 103.4 reduce-scatter.15
  1107.0 98.4 reduce-scatter.17
  1208.3 36.7 reduce-scatter.21
  1247.4 83.8 reduce-scatter.19
where the time goes:
time: 1500 us
  waiting for transfers between devices  555 us (37%)
  matrix products  404 us (27%)
  Pallas kernels  192 us (13%)
  local copies, waits for them, and re-layouts  117 us (8%)
  other arithmetic  95.6 us (6%)
  starting transfers between devices  92.4 us (6%)
  blocking collectives  29 us (2%)
  between operations  17.2 us (1%)
    all_to_all x21, waiting for transfers between devices, exchange(): return plain(lax.all_to_all(plain(x), 'ctx', 0, 0))  367 us
    reduce_scatter x6, waiting for transfers between devices, reduce_fsdp(): return lax.psum_scatter(g.astype(bf16), FS, scatter_dimension=0, tiled=True)  143 us
    all_to_all x21, starting transfers between devices, exchange(): return plain(lax.all_to_all(plain(x), 'ctx', 0, 0))  90.3 us
    dot_general x2, matrix products, local(): u = jnp.dot(n2, up_w, preferred_element_type=f32) + vector(8, layer)  72.7 us
    pallas_call x1, Pallas kernels, gather_all(): pl.pallas_call(functools.partial(gather_kernel, Z=Z, C=C, quarter=W // C)...  54.5 us
    pallas_call x4, Pallas kernels, flash_bwd(): pl.pallas_call(functools.partial(bwd_kernel, B=B, NB=NB), out_shape=jax.S...  48.1 us
    dot_general x2, matrix products, local(): jnp.einsum('rd,fd->rf', gb, down_w, preferred_element_type=f32)  39.6 us
    dot_general x2, matrix products, local(): dn2 = jnp.einsum('rf,df->rd', du, up_w, preferred_element_type=f32)  39.1 us
  transfers between devices with their start and end apart: 44, of which 29 were waited for; matrix products, arithmetic and copies ran while one was open for 34% of the time, Pallas kernels for 12%

commit v1 on v0

--- a/solution.py
+++ b/solution.py
@@ -797,6 +797,8 @@
             d_row, d_up = after(d_row, d_up)
             mine, middle_sizes = ctx_begin([fours[1], d_up, d_down])
             d_back, mine = after(d_row, mine)
+            end_a, mine = after(end_a, mine)
+            middle = ctx_end(mine)
         d_qkv = jnp.einsum("rd,rc->dc", n1, d_row, preferred_element_type=f32).astype(bf16)
         if layer:
             d_row, d_four = after(d_row, plain(jnp.concatenate([d_qkv, d_out], axis=1)))
@@ -816,16 +818,13 @@
                 (d_gain2, shard), (d_bias2, shard), (d_down_b, shard), (d_up_b, 4 * shard))], axis=1)
 
     vec_grads = jnp.stack(small, axis=1)
+    stream = end_m + jnp.dot(end_a, end_w, preferred_element_type=f32) + end_b
+    activations = (stream * live).astype(bf16)[None]
+    vec_grads, middle, activations = after(vec_grads, middle, activations)
     vec_grads = jnp.sum(lax.all_to_all(vec_grads, FS, 0, 0), axis=0)
     vec_grads = jnp.sum(lax.all_to_all(jnp.broadcast_to(vec_grads[None], (C,) + vec_grads.shape), "ctx", 0, 0), axis=0)
     end, vec_grads = after(fours[0], vec_grads)
-    mine_last, last_sizes = ctx_begin([end])
-    end_a, mine_last = after(end_a, mine_last)
-    whole = ctx_end(jnp.concatenate([mine, mine_last], axis=0))
-    stream = end_m + jnp.dot(end_a, end_w, preferred_element_type=f32) + end_b
-    activations = (stream * live).astype(bf16)[None]
-    activations, whole = after(activations, whole)
-    rest = spread((whole, middle_sizes + last_sizes), [wide_shape, wide_shape, tall_shape, wide_shape])
+    rest = spread((middle, middle_sizes), [wide_shape, wide_shape, tall_shape]) + spread(ctx_sum([end]), [wide_shape])
     matrices[1] = [rest[0]] + spread((ffn_whole, ffn_sizes), [wide_shape, tall_shape])
     matrices[0] = [rest[3], rest[1], rest[2]]
     vg = [vec_grads[:, i * shard:(i + 1) * shard] for i in range(8)] + [vec_grads[:, 8 * shard:]]

time: 1500 us -> 1480 us (0.987)
  waiting for transfers between devices: 555 us -> 269 us
  Pallas kernels: 192 us -> 377 us
  starting transfers between devices: 92.4 us -> 189 us
  blocking collectives: 29 us -> 0 us
    all_to_all x21 -> x22, waiting for transfers between devices: 367 us -> 215 us  [exchange(): return plain(lax.all_to_all(plain(x), 'ctx', 0, 0))]
    reduce_scatter x6, waiting for transfers between devices: 143 us -> 25.9 us  [reduce_fsdp(): return lax.psum_scatter(g.astype(bf16), FS, scatter_dimension=0, tiled=True)]
    pallas_call x4, Pallas kernels: 48.1 us -> 146 us  [flash_bwd(): pl.pallas_call(functools.partial(bwd_kernel, B=B, NB=NB), out_shape=jax.S...]
    pallas_call x4, Pallas kernels: 29.9 us -> 96 us  [flash_fwd(): pl.pallas_call(functools.partial(fwd_kernel, B=B, NB=NB), out_shape=(jax....]
    ppermute x9, starting transfers between devices: 0.5 us -> 59.8 us  [swap(): return lax.ppermute(x, 'core', [(0, 1), (1, 0)])]
    all_to_all x2 -> x0, blocking collectives: 29 us -> none  [the longest x1 21.6 us: local(): vec_grads = jnp.sum(lax.all_to_all(vec_grads, FS, 0, 0), axis=0)]
    all_to_all x21 -> x22, starting transfers between devices: 90.3 us -> 112 us  [exchange(): return plain(lax.all_to_all(plain(x), 'ctx', 0, 0))]
    all_to_all x0 -> x2, starting transfers between devices: none -> 16 us  [the longest x1 12.2 us: local(): vec_grads = jnp.sum(lax.all_to_all(vec_grads, FS, 0, 0), axis=0)]
  transfers between devices with their start and end apart: 44 -> 47, of which waited for: 29 -> 24; matrix products, arithmetic and copies ran while one was open for 34% -> 38% of each run, Pallas kernels for 12% -> 25%
where the time goes in v1:
time: 1480 us; the launch traced here: 1470 us
  matrix products  405 us (27%)
  Pallas kernels  377 us (25%)
  waiting for transfers between devices  269 us (18%)
  starting transfers between devices  189 us (13%)
  local copies, waits for them, and re-layouts  121 us (8%)
  other arithmetic  93.8 us (6%)
  between operations  17.1 us (1%)
    all_to_all x22, waiting for transfers between devices, exchange(): return plain(lax.all_to_all(plain(x), 'ctx', 0, 0))  215 us
    pallas_call x4, Pallas kernels, flash_bwd(): pl.pallas_call(functools.partial(bwd_kernel, B=B, NB=NB), out_shape=jax.S...  146 us
    all_to_all x22, starting transfers between devices, exchange(): return plain(lax.all_to_all(plain(x), 'ctx', 0, 0))  112 us
    pallas_call x4, Pallas kernels, flash_fwd(): pl.pallas_call(functools.partial(fwd_kernel, B=B, NB=NB), out_shape=(jax....  96 us
    dot_general x2, matrix products, local(): u = jnp.dot(n2, up_w, preferred_element_type=f32) + vector(8, layer)  72.8 us
    ppermute x9, starting transfers between devices, swap(): return lax.ppermute(x, 'core', [(0, 1), (1, 0)])  59.8 us
    pallas_call x1, Pallas kernels, gather_all(): pl.pallas_call(functools.partial(gather_kernel, Z=Z, C=C, quarter=W // C)...  54.5 us
    dot_general x2, matrix products, local(): jnp.einsum('rd,fd->rf', gb, down_w, preferred_element_type=f32)  39.7 us
  transfers between devices with their start and end apart: 47, of which 24 were waited for; matrix products, arithmetic and copies ran while one was open for 38% of the time, Pallas kernels for 25%

profile of v1, /device:TPU:0, one launch (start us, length us, event | category | flops | bytes accessed | tf_op | source)
XLA Modules:
  0.0 1471.5 jit_solution(6937629154351235625)
XLA Ops:
  30.9 54.5 %shard_map.280 = bf16[8,136,3584]{2,1,0:T(8,128)(2,1)} custom-call(bf16[136,3584]{1,0:T(8,128)(2,1)} %pad.4.x_ref), custom_call_target="tpu_custom_call" | custom-call | bytes 38993920 | tf_op jit(solution)/shard_map/pallas_call | solution.py:512
  128.3 31.5 %all-to-all-done = bf16[4,1024,384]{2,1,0:T(8,128)(2,1)S(1)} async-done(((bf16[4,1024,384]{2,1,0:T(8,128)(2,1)}), bf16[4,1024,384]{2,1,0:T(8,128)(2,1)S(1)}, u32[]{:S(2)}, u32[]{:S(2)}) %all-to-all-start) | async-done | bytes 3145760 | tf_op jit(solution)/shard_map/all_to_all | solution.py:639
  167.4 41.2 %shard_map.284 = (bf16[1,4096,128]{2,1,0:T(8,128)(2,1)S(1)}, f32[1,8,4096]{2,1,0:T(8,128)S(1)}) custom-call(s32[1,8]{1,0:T(1,128)S(1)} %bitcast.294, s32[1]{0:T(128)S(6)} %select_n.21.nb_ref, bf16[1,4096,384]{2,1,0:T(8,128)(2,1)S(1)} %bitcast.282), custom_call_target="tpu_custom_call" | custom-call | flops 8589934592 | bytes 4194304 | tf_op jit(solution)/shard_map/pallas_call | solution.py:88
  228.6 30.0 %collective-permute-start.2 = (bf16[4,1024,128]{2,1,0:T(8,128)(2,1)S(1)}, bf16[4,1024,128]{2,1,0:T(8,128)(2,1)}, u32[]{:S(2)}, u32[]{:S(2)}) collective-permute-start(bf16[4,1024,128]{2,1,0:T(8,128)(2,1)S(1)} %bitcast.298), channel_id=1, source_target_pairs={{0,4},{4,0},{1,5},{5,1},{2,6},{6,2},{3,7},{7,3},{8,12},{12,8},{9,1... | collective-permute-start | bytes 3145736 | tf_op jit(solution)/shard_map/ppermute | solution.py:579
  294.7 36.4 %add_convert_fusion.1 = (bf16[1024,4352]{1,0:T(8,128)(2,1)}, bf16[1024,4352]{1,0:T(8,128)(2,1)}) fusion(f32[4352]{0:T(1024)S(1)} %add.284, bf16[1,1088,4352]{2,1,0:T(8,128)(2,1)} %all-gather.18.cloned.1.call-done, f32[1024,1088]{0,1:T(8,128)} %copy-done.50, f32[1088]{0:T(1024)S(1)} %copy-done.102, f32[1088]{0:T(1024)S(1)} %get-tuple-element.209, ...), kind=kOutput, calls=%fused_computation.14 | convolution fusion | flops 9827581952 | bytes 31786496 | tf_op jit(solution)/shard_map/dot_general | solution.py:680
  331.2 17.8 %fusion.157 = (f32[1024]{0:T(1024)S(1)}, f32[1024,1088]{0,1:T(8,128)}) fusion(f32[1088]{0:T(1024)S(1)} %copy-done.108, f32[1024,1088]{0,1:T(8,128)} %copy-done.50, bf16[1024,4352]{1,0:T(8,128)(2,1)} %get-tuple-element.106, bf16[1,4352,1088]{2,1,0:T(8,128)(2,1)} %all-gather.20.cloned.1.call-done), kind=kOutput, calls=%fused_computation.289 | convolution fusion | flops 9700572160 | bytes 27304192 | tf_op jit(solution)/shard_map/dot_general | solution.py:686
  385.5 30.7 %all-to-all-done.4 = bf16[4,1024,384]{2,1,0:T(8,128)(2,1)S(1)} async-done(((bf16[4,1024,384]{2,1,0:T(8,128)(2,1)}), bf16[4,1024,384]{2,1,0:T(8,128)(2,1)S(1)}, u32[]{:S(2)}, u32[]{:S(2)}) %all-to-all-start.4) | async-done | bytes 3145760 | tf_op jit(solution)/shard_map/all_to_all | solution.py:639
  421.1 41.0 %shard_map.290 = (bf16[1,4096,128]{2,1,0:T(8,128)(2,1)S(1)}, f32[1,8,4096]{2,1,0:T(8,128)S(1)}) custom-call(s32[1,8]{1,0:T(1,128)S(1)} %bitcast.295, s32[1]{0:T(128)S(6)} %select_n.21.nb_ref, bf16[1,4096,384]{2,1,0:T(8,128)(2,1)S(1)} %bitcast.284), custom_call_target="tpu_custom_call" | custom-call | flops 8589934592 | bytes 4194304 | tf_op jit(solution)/shard_map/pallas_call | solution.py:88
  485.3 29.4 %collective-permute-start.4 = (bf16[4,1024,128]{2,1,0:T(8,128)(2,1)S(1)}, bf16[4,1024,128]{2,1,0:T(8,128)(2,1)}, u32[]{:S(2)}, u32[]{:S(2)}) collective-permute-start(bf16[4,1024,128]{2,1,0:T(8,128)(2,1)S(1)} %bitcast.299), channel_id=1, source_target_pairs={{0,4},{4,0},{1,5},{5,1},{2,6},{6,2},{3,7},{7,3},{8,12},{12,8},{9,1... | collective-permute-start | bytes 3145736 | tf_op jit(solution)/shard_map/ppermute | solution.py:579
  551.9 36.4 %add_convert_fusion = (bf16[1024,4352]{1,0:T(8,128)(2,1)}, bf16[1024,4352]{1,0:T(8,128)(2,1)}) fusion(f32[4352]{0:T(1024)S(1)} %add.312, bf16[1,1088,4352]{2,1,0:T(8,128)(2,1)} %all-gather.24.cloned.1.call-done, f32[1024,1088]{0,1:T(8,128)} %copy-done.39, f32[1088]{0:T(1024)S(1)} %copy-done.106, f32[1088]{0:T(1024)S(1)} %copy-done.68, ...), kind=kOutput, calls=%fused_computation.12 | convolution fusion | flops 9827581952 | bytes 31786496 | tf_op jit(solution)/shard_map/dot_general | solution.py:680
  588.3 17.6 %convolution_convert_fusion.3 = bf16[4352,1088]{1,0:T(8,128)(2,1)} fusion(bf16[1024,4352]{1,0:T(8,128)(2,1)} %get-tuple-element.173, bf16[1024,1088]{0,1:T(8,128)(2,1)S(1)} %copy-done.52), kind=kOutput, calls=%fused_computation.7 | convolution fusion | flops 9701965824 | bytes 20611072 | tf_op jit(solution)/shard_map/rf,rd->fd/dot_general | solution.py:738
  606.0 19.9 %multiply_convert_fusion.1 = bf16[1024,4352]{1,0:T(8,128)(2,1)} fusion(bf16[1024,4352]{1,0:T(8,128)(2,1)} %get-tuple-element.116, bf16[1024,1088]{0,1:T(8,128)(2,1)} %fusion.55, bf16[1,4352,1088]{2,1,0:T(8,128)(2,1)} %all-gather.26.cloned.1.call-done), kind=kOutput, calls=%fused_computation.11 | convolution fusion | flops 9710600192 | bytes 29523968 | tf_op jit(solution)/shard_map/rd,fd->rf/dot_general | solution.py:745
  625.9 16.9 %convolution_convert_fusion.2 = bf16[1088,4352]{1,0:T(8,128)(2,1)} fusion(bf16[1024,4352]{1,0:T(8,128)(2,1)} %multiply_convert_fusion.1, f32[1024,1088]{0,1:T(8,128)} %copy-done.39, f32[1088]{0:T(1024)S(1)} %copy-done.106, f32[1088]{0:T(1024)S(1)} %copy-done.68, f32[1024]{0:T(1024)S(1)} %add_rsqrt_fusion, f32[1024]{0:T(1024)S(1)} %broadcast_multiply_fusion.8), kind=kOutput, calls=%fused_computation.6 | convolution fusion | flops 9707536384 | bytes 22856192 | tf_op jit(solution)/shard_map/rd,rf->df/dot_general | solution.py:750
  644.8 19.4 %multiply_reduce_fusion = (f32[1088]{0:T(1024)}, f32[1024]{0:T(1024)S(1)}, f32[1024]{0:T(1024)S(1)}, f32[1088]{0:T(1024)}, f32[1024,1088]{0,1:T(8,128)S(1)}) fusion(f32[1024,1088]{0,1:T(8,128)} %copy-done.39, f32[1024]{0:T(1024)S(1)} %add_rsqrt_fusion, f32[1024]{0:T(1024)S(1)} %broadcast_multiply_fusion.8, f32[1088]{0:T(1024)S(1)} %copy-done.68, ...), kind=kOutput, calls=%fused_computation.72 | convolution fusion | flops 9707253760 | bytes 27325184 | tf_op jit(solution)/shard_map/rf,df->rd/dot_general | solution.py:753
  707.7 62.2 %shard_map.295 = bf16[1,4096,384]{2,1,0:T(8,128)(2,1)S(1)} custom-call(s32[1,8]{1,0:T(1,128)S(1)} %bitcast.296, s32[1]{0:T(128)S(6)} %select_n.21.nb_ref, bf16[1,4096,384]{2,1,0:T(8,128)(2,1)} %bitcast.285, bf16[1,4096,128]{2,1,0:T(8,128)(2,1)S(1)} %copy-done.7, bf16[1,4096,128]{2,1,0:T(8,128)(2,1)S(1)} %bitcast.291, f32[1,8,4096]{2,1,0:T(8,128)S(1)} %copy-done.38), custom_call_target="tpu_custom_call" | custom-call | flops 21474836480 | bytes 9830400 | tf_op jit(solution)/shard_map/pallas_call | solution.py:166
  797.2 25.9 %reduce-scatter.12.cloned.1.call-done = bf16[136,4352]{1,0:T(8,128)(2,1)} async-done(((bf16[1088,4352]{1,0:T(8,128)(2,1)}), bf16[136,4352]{1,0:T(8,128)(2,1)}) %reduce-scatter.12.cloned.1.call-update) | async-done | bytes 1183760 | tf_op jit(solution)/shard_map/reduce_scatter | solution.py:690
  851.3 19.1 %all-to-all-done.11.refs_1_ = bf16[4,1024,384]{2,1,0:T(8,128)(2,1)} async-done(((bf16[4,1024,384]{2,1,0:T(8,128)(2,1)}), bf16[4,1024,384]{2,1,0:T(8,128)(2,1)}, u32[]{:S(2)}, u32[]{:S(2)}) %all-to-all-start.11) | async-done | bytes 3145760 | tf_op jit(solution)/shard_map/all_to_all | solution.py:639
  947.2 19.8 %multiply_convert_fusion = bf16[1024,4352]{1,0:T(8,128)(2,1)} fusion(bf16[1024,4352]{1,0:T(8,128)(2,1)} %get-tuple-element.136, bf16[1024,1088]{0,1:T(8,128)(2,1)} %copy-done.51, bf16[1,4352,1088]{2,1,0:T(8,128)(2,1)} %all-gather.20.cloned.1.call-done), kind=kOutput, calls=%fused_computation.10 | convolution fusion | flops 9710600192 | bytes 29523968 | tf_op jit(solution)/shard_map/rd,fd->rf/dot_general | solution.py:745
  976.3 17.0 %convolution_convert_fusion = bf16[1088,4352]{1,0:T(8,128)(2,1)} fusion(bf16[1024,4352]{1,0:T(8,128)(2,1)} %multiply_convert_fusion, f32[1024,1088]{0,1:T(8,128)} %copy-done.50, f32[1088]{0:T(1024)S(1)} %copy-done.103, f32[1088]{0:T(1024)S(1)} %copy-done.85, f32[1024]{0:T(1024)S(1)} %copy-done.98, f32[1024]{0:T(1024)S(1)} %copy-done.78), kind=kOutput, calls=%fused_computation.4 | convolution fusion | flops 9707536384 | bytes 22856192 | tf_op jit(solution)/shard_map/rd,rf->df/dot_general | solution.py:750
  1003.2 19.0 %multiply_reduce_fusion.2 = (f32[1088]{0:T(1024)}, f32[1024]{0:T(1024)S(1)}, f32[1024]{0:T(1024)S(1)}, f32[1088]{0:T(1024)}, f32[1024,1088]{0,1:T(8,128)S(1)}) fusion(f32[1024,1088]{0,1:T(8,128)} %copy-done.50, f32[1024]{0:T(1024)S(1)} %copy-done.98, f32[1024]{0:T(1024)S(1)} %copy-done.78, f32[1088]{0:T(1024)S(1)} %copy-done.85, ...), kind=kOutput, calls=%fused_computation.74 | convolution fusion | flops 9707253760 | bytes 27325184 | tf_op jit(solution)/shard_map/rf,df->rd/dot_general | solution.py:753
  1071.1 62.2 %shard_map.299 = bf16[1,4096,384]{2,1,0:T(8,128)(2,1)S(1)} custom-call(s32[1,8]{1,0:T(1,128)S(1)} %bitcast.297, s32[1]{0:T(128)S(6)} %select_n.21.nb_ref, bf16[1,4096,384]{2,1,0:T(8,128)(2,1)} %bitcast.283, bf16[1,4096,128]{2,1,0:T(8,128)(2,1)S(1)} %copy-done.5, bf16[1,4096,128]{2,1,0:T(8,128)(2,1)S(1)} %bitcast.290, f32[1,8,4096]{2,1,0:T(8,128)S(1)} %copy-done.36), custom_call_target="tpu_custom_call" | custom-call | flops 21474836480 | bytes 9830400 | tf_op jit(solution)/shard_map/pallas_call | solution.py:166
  1181.9 26.2 %all-to-all-done.17.refs_1_ = bf16[4,1024,384]{2,1,0:T(8,128)(2,1)} async-done(((bf16[4,1024,384]{2,1,0:T(8,128)(2,1)}), bf16[4,1024,384]{2,1,0:T(8,128)(2,1)}, u32[]{:S(2)}, u32[]{:S(2)}) %all-to-all-start.17) | async-done | bytes 3145760 | tf_op jit(solution)/shard_map/all_to_all | solution.py:639
  1279.4 28.9 %all-to-all-done.18 = bf16[4,408,1088]{2,1,0:T(8,128)(2,1)} async-done(((bf16[4,408,1088]{2,1,0:T(8,128)(2,1)}), bf16[4,408,1088]{2,1,0:T(8,128)(2,1)}, u32[]{:S(2)}, u32[]{:S(2)}) %all-to-all-start.18) | async-done | bytes 3551264 | tf_op jit(solution)/shard_map/all_to_all | solution.py:639
  1340.4 17.4 %fusion.59 = bf16[1,1024,1088]{1,2,0:T(8,128)(2,1)} fusion(f32[1024,1088]{0,1:T(8,128)} %copy-done.39, bf16[1024,4352]{1,0:T(8,128)(2,1)} %get-tuple-element.173, bf16[1,4352,1088]{2,1,0:T(8,128)(2,1)} %all-gather.26.cloned.1.call-done, f32[1088]{0:T(1024)S(1)} %copy-done.99, f32[1024]{0:T(1024)S(1)} %bitcast.334), kind=kOutput, calls=%fused_computation.98 | convolution fusion | flops 9701687296 | bytes 25075968 | tf_op jit(solution)/shard_map/dot_general | solution.py:821
  (608 shorter events, 733.9 us)
Async XLA Ops:
  7.2 278.8 %all-gather.16.cloned.1.call-start = ((), (), s32[]{:S(2)}) async-start(), calls=%async_computation.38 | async-start | bytes 2820096 | tf_op jit(solution)/shard_map/all_gather | solution.py:605
  9.5 285.2 %all-gather.18.cloned.1.call-start = ((), (), s32[]{:S(2)}) async-start(), calls=%async_computation.39 | async-start | bytes 10653696 | tf_op jit(solution)/shard_map/all_gather | solution.py:605
  13.7 317.5 %all-gather.20.cloned.1.call-start = ((), (), s32[]{:S(2)}) async-start(), calls=%async_computation.40 | async-start | bytes 11280384 | tf_op jit(solution)/shard_map/all_gather | solution.py:605
  18.1 333.7 %all-gather.14.cloned.1.call-start = ((), (), s32[]{:S(2)}) async-start(), calls=%async_computation.31 | async-start | bytes 8146944 | tf_op jit(solution)/shard_map/all_gather | solution.py:605
  119.3 40.5 %all-to-all-start = ((bf16[4,1024,384]{2,1,0:T(8,128)(2,1)}), bf16[4,1024,384]{2,1,0:T(8,128)(2,1)S(1)}, u32[]{:S(2)}, u32[]{:S(2)}) async-start(bf16[4,1024,384]{2,1,0:T(8,128)(2,1)} %shard_map.282), calls=%async_computation | async-start | bytes 6291456 | tf_op jit(solution)/shard_map/all_to_all | solution.py:639
  123.1 418.9 %all-gather.22.cloned.1.call-start = ((), (), s32[]{:S(2)}) async-start(), calls=%async_computation.41 | async-start | bytes 2820096 | tf_op jit(solution)/shard_map/all_gather | solution.py:605
  159.8 52.3 %all-to-all-start.1 = ((bf16[4,1024,512]{2,1,0:T(8,128)(2,1)}), bf16[4,1024,512]{2,1,0:T(8,128)(2,1)}, u32[]{:S(2)}, u32[]{:S(2)}) async-start(bf16[4,1024,512]{2,1,0:T(8,128)(2,1)} %pad_maximum_fusion.1), calls=%async_computation.1 | async-start | bytes 8388608 | tf_op jit(solution)/shard_map/all_to_all | solution.py:639
  164.7 387.1 %all-gather.24.cloned.1.call-start = ((), (), s32[]{:S(2)}) async-start(), calls=%async_computation.42 | async-start | bytes 10653696 | tf_op jit(solution)/shard_map/all_gather | solution.py:605
  375.5 40.7 %all-to-all-start.4 = ((bf16[4,1024,384]{2,1,0:T(8,128)(2,1)}), bf16[4,1024,384]{2,1,0:T(8,128)(2,1)S(1)}, u32[]{:S(2)}, u32[]{:S(2)}) async-start(bf16[4,1024,384]{2,1,0:T(8,128)(2,1)} %shard_map.288), calls=%async_computation.4 | async-start | bytes 6291456 | tf_op jit(solution)/shard_map/all_to_all | solution.py:639
  379.2 226.8 %all-gather.26.cloned.1.call-start = ((), (), s32[]{:S(2)}) async-start(), calls=%async_computation.43 | async-start | bytes 11280384 | tf_op jit(solution)/shard_map/all_gather | solution.py:605
  416.2 52.5 %all-to-all-start.5 = ((bf16[4,1024,512]{2,1,0:T(8,128)(2,1)}), bf16[4,1024,512]{2,1,0:T(8,128)(2,1)}, u32[]{:S(2)}, u32[]{:S(2)}) async-start(bf16[4,1024,512]{2,1,0:T(8,128)(2,1)} %pad_maximum_fusion.2), calls=%async_computation.5 | async-start | bytes 8388608 | tf_op jit(solution)/shard_map/all_to_all | solution.py:639
  521.4 275.8 %reduce-scatter.10.cloned.1.call-start = ((), (), s32[]{:S(2)}) async-start(), calls=%async_computation.32 | async-start | bytes 11280384 | tf_op jit(solution)/shard_map/reduce_scatter | solution.py:690
  605.9 217.2 %reduce-scatter.12.cloned.1.call-start = ((), (), s32[]{:S(2)}) async-start(), calls=%async_computation.33 | async-start | bytes 10653696 | tf_op jit(solution)/shard_map/reduce_scatter | solution.py:690
  695.1 76.5 %all-to-all-start.9 = ((bf16[4,1024,256]{2,1,0:T(8,128)(2,1)}), bf16[4,1024,256]{2,1,0:T(8,128)(2,1)S(1)}, u32[]{:S(2)}, u32[]{:S(2)}) async-start(bf16[4,1024,256]{2,1,0:T(8,128)(2,1)} %pad_maximum_fusion.6), calls=%async_computation.9 | async-start | bytes 4194304 | tf_op jit(solution)/shard_map/all_to_all | solution.py:639
  829.1 41.4 %all-to-all-start.11 = ((bf16[4,1024,384]{2,1,0:T(8,128)(2,1)}), bf16[4,1024,384]{2,1,0:T(8,128)(2,1)}, u32[]{:S(2)}, u32[]{:S(2)}) async-start(bf16[4,1024,384]{2,1,0:T(8,128)(2,1)} %collective-permute-done.6), calls=%async_computation.13 | async-start | bytes 6291456 | tf_op jit(solution)/shard_map/all_to_all | solution.py:639
  833.7 225.7 %reduce-scatter.14.cloned.1.call-start = ((), (), s32[]{:S(2)}) async-start(), calls=%async_computation.34 | async-start | bytes 10653696 | tf_op jit(solution)/shard_map/reduce_scatter | solution.py:690
  897.7 262.8 %reduce-scatter.16.cloned.1.call-start = ((), (), s32[]{:S(2)}) async-start(), calls=%async_computation.35 | async-start | bytes 11280384 | tf_op jit(solution)/shard_map/reduce_scatter | solution.py:690
  947.0 269.9 %reduce-scatter.18.cloned.1.call-start = ((), (), s32[]{:S(2)}) async-start(), calls=%async_computation.36 | async-start | bytes 10653696 | tf_op jit(solution)/shard_map/reduce_scatter | solution.py:690
  1059.5 75.6 %all-to-all-start.15 = ((bf16[4,1024,256]{2,1,0:T(8,128)(2,1)}), bf16[4,1024,256]{2,1,0:T(8,128)(2,1)S(1)}, u32[]{:S(2)}, u32[]{:S(2)}) async-start(bf16[4,1024,256]{2,1,0:T(8,128)(2,1)} %pad_maximum_fusion.7), calls=%async_computation.18 | async-start | bytes 4194304 | tf_op jit(solution)/shard_map/all_to_all | solution.py:639
  1139.8 101.1 %reduce-scatter.22.cloned.1.call-start = ((), (), s32[]{:S(2)}) async-start(), calls=%async_computation.44 | async-start | bytes 2820096
  1166.6 41.4 %all-to-all-start.17 = ((bf16[4,1024,384]{2,1,0:T(8,128)(2,1)}), bf16[4,1024,384]{2,1,0:T(8,128)(2,1)}, u32[]{:S(2)}, u32[]{:S(2)}) async-start(bf16[4,1024,384]{2,1,0:T(8,128)(2,1)} %collective-permute-done.8), calls=%async_computation.21 | async-start | bytes 6291456 | tf_op jit(solution)/shard_map/all_to_all | solution.py:639
  1171.2 228.9 %reduce-scatter.20.cloned.1.call-start = ((), (), s32[]{:S(2)}) async-start(), calls=%async_computation.37 | async-start | bytes 8146944 | tf_op jit(solution)/shard_map/reduce_scatter | solution.py:690
  1263.1 45.2 %all-to-all-start.18 = ((bf16[4,408,1088]{2,1,0:T(8,128)(2,1)}), bf16[4,408,1088]{2,1,0:T(8,128)(2,1)}, u32[]{:S(2)}, u32[]{:S(2)}) async-start(bf16[4,408,1088]{2,1,0:T(8,128)(2,1)} %pad_maximum_fusion.3), calls=%async_computation.23 | async-start | bytes 7520256 | tf_op jit(solution)/shard_map/all_to_all | solution.py:639
  1313.7 47.5 %all-to-all-start.19 = ((bf16[4,408,1088]{2,1,0:T(8,128)(2,1)}), bf16[4,408,1088]{2,1,0:T(8,128)(2,1)}, u32[]{:S(2)}, u32[]{:S(2)}) async-start(bf16[4,408,1088]{2,1,0:T(8,128)(2,1)} %broadcast_in_dim.48), calls=%async_computation.24 | async-start | bytes 7520256 | tf_op jit(solution)/shard_map/all_to_all | solution.py:639
  (153 other events, 3474.8 us)
Sparse Core Ops, SparseCore 0:
  9.7 48.8 all-gather.15
  60.8 89.6 all-gather.17
  152.7 94.0 all-gather.19
  248.9 70.9 all-gather.13
  321.4 31.4 all-gather.21
  354.4 90.0 all-gather.23
  446.7 94.0 all-gather.25
  606.1 116.1 reduce-scatter.9
  724.6 98.4 reduce-scatter.11
  897.8 97.5 reduce-scatter.13
  997.7 103.4 reduce-scatter.15
  1103.3 98.4 reduce-scatter.17
  1204.1 36.7 reduce-scatter.21
  1243.2 81.2 reduce-scatter.19

commit v2 on v1

--- a/solution.py
+++ b/solution.py
@@ -544,13 +544,12 @@
 
 
 def gelu_parts(u):
-    z = jnp.abs(u) * 0.7071067811865476
-    t = 1.0 / (1.0 + 0.3275911 * z)
-    e = jnp.exp(-z * z)
-    poly = t * (0.254829592 + t * (-0.284496736 + t * (1.421413741 + t * (-1.453152027 + t * 1.061405429))))
-    half = 0.5 * poly * e
+    t = 1.0 / (1.0 + 0.2316418882 * jnp.abs(u))
+    e = jnp.exp2(u * u * -0.7213475204444817)
+    poly = 0.127414796 + t * (-0.142248368 + t * (0.7107068705 + t * (-0.7265760135 + t * 0.5307027145)))
+    half = e * (t * poly)
     cdf = jnp.where(u >= 0, 1.0 - half, half)
-    return u * cdf, cdf + u * e * 0.3989422804014327
+    return u * cdf, cdf + (u * 0.3989422804014327) * e
 
 
 def local(

time: 1480 us -> 1510 us (1.020)
  Pallas kernels: 377 us -> 551 us
  starting transfers between devices: 189 us -> 116 us
  waiting for transfers between devices: 269 us -> 213 us
    pallas_call x4, Pallas kernels: 146 us -> 254 us  [flash_bwd(): pl.pallas_call(functools.partial(bwd_kernel, B=B, NB=NB), out_shape=jax.S...]
    pallas_call x4, Pallas kernels: 96 us -> 169 us  [flash_fwd(): pl.pallas_call(functools.partial(fwd_kernel, B=B, NB=NB), out_shape=(jax....]
    ppermute x9, starting transfers between devices: 59.8 us -> 0.59 us  [swap(): return lax.ppermute(x, 'core', [(0, 1), (1, 0)])]
    reduce_scatter x6, waiting for transfers between devices: 25.9 us -> 0.01 us  [reduce_fsdp(): return lax.psum_scatter(g.astype(bf16), FS, scatter_dimension=0, tiled=True)]
    all_to_all x22, waiting for transfers between devices: 215 us -> 194 us  [exchange(): return plain(lax.all_to_all(plain(x), 'ctx', 0, 0))]
  transfers between devices with their start and end apart: 47 -> 47, of which waited for: 24 -> 20; matrix products, arithmetic and copies ran while one was open for 38% -> 36% of each run, Pallas kernels for 25% -> 36%
where the time goes in v2:
time: 1510 us; the launch traced here: 1520 us
  Pallas kernels  551 us (36%)
  matrix products  403 us (27%)
  waiting for transfers between devices  213 us (14%)
  local copies, waits for them, and re-layouts  121 us (8%)
  starting transfers between devices  116 us (8%)
  other arithmetic  93.8 us (6%)
  between operations  17.1 us (1%)
    pallas_call x4, Pallas kernels, flash_bwd(): pl.pallas_call(functools.partial(bwd_kernel, B=B, NB=NB), out_shape=jax.S...  254 us
    all_to_all x22, waiting for transfers between devices, exchange(): return plain(lax.all_to_all(plain(x), 'ctx', 0, 0))  194 us
    pallas_call x4, Pallas kernels, flash_fwd(): pl.pallas_call(functools.partial(fwd_kernel, B=B, NB=NB), out_shape=(jax....  169 us
    all_to_all x22, starting transfers between devices, exchange(): return plain(lax.all_to_all(plain(x), 'ctx', 0, 0))  107 us
    dot_general x2, matrix products, local(): u = jnp.dot(n2, up_w, preferred_element_type=f32) + vector(8, layer)  70.4 us
    pallas_call x1, Pallas kernels, gather_all(): pl.pallas_call(functools.partial(gather_kernel, Z=Z, C=C, quarter=W // C)...  54.5 us
    dot_general x2, matrix products, local(): jnp.einsum('rd,fd->rf', gb, down_w, preferred_element_type=f32)  39.7 us
    dot_general x2, matrix products, local(): dn2 = jnp.einsum('rf,df->rd', du, up_w, preferred_element_type=f32)  38.5 us
  transfers between devices with their start and end apart: 47, of which 20 were waited for; matrix products, arithmetic and copies ran while one was open for 36% of the time, Pallas kernels for 36%

profile of v2, /device:TPU:0, one launch (start us, length us, event | category | flops | bytes accessed | tf_op | source)
XLA Modules:
  0.0 1515.6 jit_solution(3346835454067538615)
XLA Ops:
  30.9 54.5 %shard_map.280 = bf16[8,136,3584]{2,1,0:T(8,128)(2,1)} custom-call(bf16[136,3584]{1,0:T(8,128)(2,1)} %pad.4.x_ref), custom_call_target="tpu_custom_call" | custom-call | bytes 38993920 | tf_op jit(solution)/shard_map/pallas_call | solution.py:512
  128.3 31.5 %all-to-all-done = bf16[4,1024,384]{2,1,0:T(8,128)(2,1)S(1)} async-done(((bf16[4,1024,384]{2,1,0:T(8,128)(2,1)}), bf16[4,1024,384]{2,1,0:T(8,128)(2,1)S(1)}, u32[]{:S(2)}, u32[]{:S(2)}) %all-to-all-start) | async-done | bytes 3145760 | tf_op jit(solution)/shard_map/all_to_all | solution.py:638
  167.4 41.2 %shard_map.284 = (bf16[1,4096,128]{2,1,0:T(8,128)(2,1)S(1)}, f32[1,8,4096]{2,1,0:T(8,128)S(1)}) custom-call(s32[1,8]{1,0:T(1,128)S(1)} %bitcast.294, s32[1]{0:T(128)S(6)} %select_n.21.nb_ref, bf16[1,4096,384]{2,1,0:T(8,128)(2,1)S(1)} %bitcast.282), custom_call_target="tpu_custom_call" | custom-call | flops 8589934592 | bytes 4194304 | tf_op jit(solution)/shard_map/pallas_call | solution.py:88
  215.6 43.3 %shard_map.283 = (bf16[1,4096,128]{2,1,0:T(8,128)(2,1)S(1)}, f32[1,8,4096]{2,1,0:T(8,128)S(1)}) custom-call(s32[1,8]{1,0:T(1,128)S(1)} %slice_bitcast_fusion.10.inv_ref, s32[1]{0:T(128)} %slice.947.nb_ref, bf16[1,4096,512]{2,1,0:T(8,128)(2,1)} %bitcast.18.x_ref), custom_call_target="tpu_custom_call" | custom-call | flops 8589934592 | bytes 4194304 | tf_op jit(solution)/shard_map/pallas_call | solution.py:88
  296.1 35.1 %add_convert_fusion.1 = (bf16[1024,4352]{1,0:T(8,128)(2,1)}, bf16[1024,4352]{1,0:T(8,128)(2,1)}) fusion(f32[4352]{0:T(1024)S(1)} %add.284, bf16[1,1088,4352]{2,1,0:T(8,128)(2,1)} %all-gather.18.cloned.1.call-done, f32[1024,1088]{0,1:T(8,128)} %copy-done.50, f32[1088]{0:T(1024)S(1)} %copy-done.102, f32[1088]{0:T(1024)S(1)} %get-tuple-element.209, ...), kind=kOutput, calls=%fused_computation.11 | convolution fusion | flops 9818669056 | bytes 31786496 | tf_op jit(solution)/shard_map/dot_general | solution.py:679
  331.3 17.8 %fusion.155 = (f32[1024]{0:T(1024)S(1)}, f32[1024,1088]{0,1:T(8,128)}) fusion(f32[1088]{0:T(1024)S(1)} %copy-done.108, f32[1024,1088]{0,1:T(8,128)} %copy-done.50, bf16[1024,4352]{1,0:T(8,128)(2,1)} %get-tuple-element.106, bf16[1,4352,1088]{2,1,0:T(8,128)(2,1)} %all-gather.20.cloned.1.call-done), kind=kOutput, calls=%fused_computation.287 | convolution fusion | flops 9700572160 | bytes 27304192 | tf_op jit(solution)/shard_map/dot_general | solution.py:685
  385.6 30.7 %all-to-all-done.4 = bf16[4,1024,384]{2,1,0:T(8,128)(2,1)S(1)} async-done(((bf16[4,1024,384]{2,1,0:T(8,128)(2,1)}), bf16[4,1024,384]{2,1,0:T(8,128)(2,1)S(1)}, u32[]{:S(2)}, u32[]{:S(2)}) %all-to-all-start.4) | async-done | bytes 3145760 | tf_op jit(solution)/shard_map/all_to_all | solution.py:638
  421.2 41.0 %shard_map.290 = (bf16[1,4096,128]{2,1,0:T(8,128)(2,1)S(1)}, f32[1,8,4096]{2,1,0:T(8,128)S(1)}) custom-call(s32[1,8]{1,0:T(1,128)S(1)} %bitcast.295, s32[1]{0:T(128)S(6)} %select_n.21.nb_ref, bf16[1,4096,384]{2,1,0:T(8,128)(2,1)S(1)} %bitcast.284), custom_call_target="tpu_custom_call" | custom-call | flops 8589934592 | bytes 4194304 | tf_op jit(solution)/shard_map/pallas_call | solution.py:88
  472.3 43.4 %shard_map.289 = (bf16[1,4096,128]{2,1,0:T(8,128)(2,1)S(1)}, f32[1,8,4096]{2,1,0:T(8,128)S(1)}) custom-call(s32[1,8]{1,0:T(1,128)S(1)} %slice_bitcast_fusion.10.inv_ref, s32[1]{0:T(128)} %slice.947.nb_ref, bf16[1,4096,512]{2,1,0:T(8,128)(2,1)} %bitcast.32.x_ref), custom_call_target="tpu_custom_call" | custom-call | flops 8589934592 | bytes 4194304 | tf_op jit(solution)/shard_map/pallas_call | solution.py:88
  553.3 35.3 %add_convert_fusion = (bf16[1024,4352]{1,0:T(8,128)(2,1)}, bf16[1024,4352]{1,0:T(8,128)(2,1)}) fusion(f32[4352]{0:T(1024)S(1)} %add.312, bf16[1,1088,4352]{2,1,0:T(8,128)(2,1)} %all-gather.24.cloned.1.call-done, f32[1024,1088]{0,1:T(8,128)} %copy-done.39, f32[1088]{0:T(1024)S(1)} %copy-done.106, f32[1088]{0:T(1024)S(1)} %copy-done.68, ...), kind=kOutput, calls=%fused_computation.8 | convolution fusion | flops 9818669056 | bytes 31786496 | tf_op jit(solution)/shard_map/dot_general | solution.py:679
  588.6 17.6 %convolution_convert_fusion.3 = bf16[4352,1088]{1,0:T(8,128)(2,1)} fusion(bf16[1024,4352]{1,0:T(8,128)(2,1)} %get-tuple-element.173, bf16[1024,1088]{0,1:T(8,128)(2,1)S(1)} %copy-done.52), kind=kOutput, calls=%fused_computation.5 | convolution fusion | flops 9701965824 | bytes 20611072 | tf_op jit(solution)/shard_map/rf,rd->fd/dot_general | solution.py:737
  606.3 19.9 %multiply_convert_fusion.1 = bf16[1024,4352]{1,0:T(8,128)(2,1)} fusion(bf16[1024,4352]{1,0:T(8,128)(2,1)} %get-tuple-element.116, bf16[1024,1088]{0,1:T(8,128)(2,1)} %fusion.53, bf16[1,4352,1088]{2,1,0:T(8,128)(2,1)} %all-gather.26.cloned.1.call-done), kind=kOutput, calls=%fused_computation.7 | convolution fusion | flops 9710600192 | bytes 29523968 | tf_op jit(solution)/shard_map/rd,fd->rf/dot_general | solution.py:744
  626.1 17.0 %convolution_convert_fusion.2 = bf16[1088,4352]{1,0:T(8,128)(2,1)} fusion(bf16[1024,4352]{1,0:T(8,128)(2,1)} %multiply_convert_fusion.1, f32[1024,1088]{0,1:T(8,128)} %copy-done.39, f32[1088]{0:T(1024)S(1)} %copy-done.106, f32[1088]{0:T(1024)S(1)} %copy-done.68, f32[1024]{0:T(1024)S(1)} %add_rsqrt_fusion, f32[1024]{0:T(1024)S(1)} %broadcast_multiply_fusion.8), kind=kOutput, calls=%fused_computation.4 | convolution fusion | flops 9707536384 | bytes 22856192 | tf_op jit(solution)/shard_map/rd,rf->df/dot_general | solution.py:749
  645.2 19.4 %multiply_reduce_fusion = (f32[1088]{0:T(1024)}, f32[1024]{0:T(1024)S(1)}, f32[1024]{0:T(1024)S(1)}, f32[1088]{0:T(1024)}, f32[1024,1088]{0,1:T(8,128)S(1)}) fusion(f32[1024,1088]{0,1:T(8,128)} %copy-done.39, f32[1024]{0:T(1024)S(1)} %add_rsqrt_fusion, f32[1024]{0:T(1024)S(1)} %broadcast_multiply_fusion.8, f32[1088]{0:T(1024)S(1)} %copy-done.68, ...), kind=kOutput, calls=%fused_computation.70 | convolution fusion | flops 9707253760 | bytes 27325184 | tf_op jit(solution)/shard_map/rf,df->rd/dot_general | solution.py:752
  705.0 62.2 %shard_map.295 = bf16[1,4096,384]{2,1,0:T(8,128)(2,1)S(1)} custom-call(s32[1,8]{1,0:T(1,128)S(1)} %bitcast.296, s32[1]{0:T(128)S(6)} %select_n.21.nb_ref, bf16[1,4096,384]{2,1,0:T(8,128)(2,1)} %bitcast.285, bf16[1,4096,128]{2,1,0:T(8,128)(2,1)S(1)} %copy-done.7, bf16[1,4096,128]{2,1,0:T(8,128)(2,1)S(1)} %bitcast.291, f32[1,8,4096]{2,1,0:T(8,128)S(1)} %copy-done.38), custom_call_target="tpu_custom_call" | custom-call | flops 21474836480 | bytes 9830400 | tf_op jit(solution)/shard_map/pallas_call | solution.py:166
  774.7 64.7 %shard_map.294 = bf16[1,4096,384]{2,1,0:T(8,128)(2,1)} custom-call(s32[1,8]{1,0:T(1,128)S(1)} %copy-done.30, s32[1]{0:T(128)} %slice.947.nb_ref, bf16[1,4096,512]{2,1,0:T(8,128)(2,1)} %bitcast.32.x_ref, bf16[1,4096,128]{2,1,0:T(8,128)(2,1)S(1)} %copy-done.28, bf16[1,4096,256]{2,1,0:T(8,128)(2,1)S(1)} %bitcast.281, f32[1,8,4096]{2,1,0:T(8,128)S(1)} %copy-done.34), custom_call_target="tpu_custom_call" | custom-call | flops 21474836480 | bytes 9830400 | tf_op jit(solution)/shard_map/pallas_call | solution.py:166
  867.7 19.9 %all-to-all-done.11.refs_1_ = bf16[4,1024,384]{2,1,0:T(8,128)(2,1)} async-done(((bf16[4,1024,384]{2,1,0:T(8,128)(2,1)}), bf16[4,1024,384]{2,1,0:T(8,128)(2,1)}, u32[]{:S(2)}, u32[]{:S(2)}) %all-to-all-start.11) | async-done | bytes 3145760 | tf_op jit(solution)/shard_map/all_to_all | solution.py:638
  964.3 19.8 %multiply_convert_fusion = bf16[1024,4352]{1,0:T(8,128)(2,1)} fusion(bf16[1024,4352]{1,0:T(8,128)(2,1)} %get-tuple-element.136, bf16[1024,1088]{0,1:T(8,128)(2,1)} %copy-done.51, bf16[1,4352,1088]{2,1,0:T(8,128)(2,1)} %all-gather.20.cloned.1.call-done), kind=kOutput, calls=%fused_computation.6 | convolution fusion | flops 9710600192 | bytes 29523968 | tf_op jit(solution)/shard_map/rd,fd->rf/dot_general | solution.py:744
  1021.2 19.0 %multiply_reduce_fusion.2 = (f32[1088]{0:T(1024)}, f32[1024]{0:T(1024)S(1)}, f32[1024]{0:T(1024)S(1)}, f32[1088]{0:T(1024)}, f32[1024,1088]{0,1:T(8,128)S(1)}) fusion(f32[1024,1088]{0,1:T(8,128)} %copy-done.50, f32[1024]{0:T(1024)S(1)} %copy-done.98, f32[1024]{0:T(1024)S(1)} %copy-done.78, f32[1088]{0:T(1024)S(1)} %copy-done.85, ...), kind=kOutput, calls=%fused_computation.72 | convolution fusion | flops 9707253760 | bytes 27325184 | tf_op jit(solution)/shard_map/rf,df->rd/dot_general | solution.py:752
  1087.2 62.2 %shard_map.299 = bf16[1,4096,384]{2,1,0:T(8,128)(2,1)S(1)} custom-call(s32[1,8]{1,0:T(1,128)S(1)} %bitcast.297, s32[1]{0:T(128)S(6)} %select_n.21.nb_ref, bf16[1,4096,384]{2,1,0:T(8,128)(2,1)} %bitcast.283, bf16[1,4096,128]{2,1,0:T(8,128)(2,1)S(1)} %copy-done.5, bf16[1,4096,128]{2,1,0:T(8,128)(2,1)S(1)} %bitcast.290, f32[1,8,4096]{2,1,0:T(8,128)S(1)} %copy-done.36), custom_call_target="tpu_custom_call" | custom-call | flops 21474836480 | bytes 9830400 | tf_op jit(solution)/shard_map/pallas_call | solution.py:166
  1156.0 64.6 %shard_map.298 = bf16[1,4096,384]{2,1,0:T(8,128)(2,1)} custom-call(s32[1,8]{1,0:T(1,128)S(1)} %copy-done.30, s32[1]{0:T(128)} %slice.947.nb_ref, bf16[1,4096,512]{2,1,0:T(8,128)(2,1)} %bitcast.18.x_ref, bf16[1,4096,128]{2,1,0:T(8,128)(2,1)S(1)} %copy-done.26, bf16[1,4096,256]{2,1,0:T(8,128)(2,1)S(1)} %bitcast.280, f32[1,8,4096]{2,1,0:T(8,128)S(1)} %copy-done.32), custom_call_target="tpu_custom_call" | custom-call | flops 21474836480 | bytes 9830400 | tf_op jit(solution)/shard_map/pallas_call | solution.py:166
  1241.9 26.8 %all-to-all-done.17.refs_1_ = bf16[4,1024,384]{2,1,0:T(8,128)(2,1)} async-done(((bf16[4,1024,384]{2,1,0:T(8,128)(2,1)}), bf16[4,1024,384]{2,1,0:T(8,128)(2,1)}, u32[]{:S(2)}, u32[]{:S(2)}) %all-to-all-start.17) | async-done | bytes 3145760 | tf_op jit(solution)/shard_map/all_to_all | solution.py:638
  1330.3 31.0 %all-to-all-done.18 = bf16[4,408,1088]{2,1,0:T(8,128)(2,1)} async-done(((bf16[4,408,1088]{2,1,0:T(8,128)(2,1)}), bf16[4,408,1088]{2,1,0:T(8,128)(2,1)}, u32[]{:S(2)}, u32[]{:S(2)}) %all-to-all-start.18) | async-done | bytes 3551264 | tf_op jit(solution)/shard_map/all_to_all | solution.py:638
  1393.3 17.4 %fusion.57 = bf16[1,1024,1088]{1,2,0:T(8,128)(2,1)} fusion(f32[1024,1088]{0,1:T(8,128)} %copy-done.39, bf16[1024,4352]{1,0:T(8,128)(2,1)} %get-tuple-element.173, bf16[1,4352,1088]{2,1,0:T(8,128)(2,1)} %all-gather.26.cloned.1.call-done, f32[1088]{0:T(1024)S(1)} %copy-done.99, f32[1024]{0:T(1024)S(1)} %bitcast.334), kind=kOutput, calls=%fused_computation.96 | convolution fusion | flops 9701687296 | bytes 25075968 | tf_op jit(solution)/shard_map/dot_general | solution.py:820
  (608 shorter events, 663.1 us)
Async XLA Ops:
  7.2 280.2 %all-gather.16.cloned.1.call-start = ((), (), s32[]{:S(2)}) async-start(), calls=%async_computation.38 | async-start | bytes 2820096 | tf_op jit(solution)/shard_map/all_gather | solution.py:604
  9.5 286.5 %all-gather.18.cloned.1.call-start = ((), (), s32[]{:S(2)}) async-start(), calls=%async_computation.39 | async-start | bytes 10653696 | tf_op jit(solution)/shard_map/all_gather | solution.py:604
  13.7 317.5 %all-gather.20.cloned.1.call-start = ((), (), s32[]{:S(2)}) async-start(), calls=%async_computation.40 | async-start | bytes 11280384 | tf_op jit(solution)/shard_map/all_gather | solution.py:604
  18.1 333.8 %all-gather.14.cloned.1.call-start = ((), (), s32[]{:S(2)}) async-start(), calls=%async_computation.31 | async-start | bytes 8146944 | tf_op jit(solution)/shard_map/all_gather | solution.py:604
  123.1 420.3 %all-gather.22.cloned.1.call-start = ((), (), s32[]{:S(2)}) async-start(), calls=%async_computation.41 | async-start | bytes 2820096 | tf_op jit(solution)/shard_map/all_gather | solution.py:604
  159.8 52.3 %all-to-all-start.1 = ((bf16[4,1024,512]{2,1,0:T(8,128)(2,1)}), bf16[4,1024,512]{2,1,0:T(8,128)(2,1)}, u32[]{:S(2)}, u32[]{:S(2)}) async-start(bf16[4,1024,512]{2,1,0:T(8,128)(2,1)} %pad_maximum_fusion.1), calls=%async_computation.1 | async-start | bytes 8388608 | tf_op jit(solution)/shard_map/all_to_all | solution.py:638
  164.7 388.5 %all-gather.24.cloned.1.call-start = ((), (), s32[]{:S(2)}) async-start(), calls=%async_computation.42 | async-start | bytes 10653696 | tf_op jit(solution)/shard_map/all_gather | solution.py:604
  212.0 47.5 %all-to-all-start.2 = ((bf16[4,1024,128]{2,1,0:T(8,128)(2,1)}), bf16[4,1024,128]{2,1,0:T(8,128)(2,1)S(1)}, u32[]{:S(2)}, u32[]{:S(2)}) async-start(bf16[4,1024,128]{2,1,0:T(8,128)(2,1)} %bitcast.288), calls=%async_computation.2 | async-start | bytes 2097152 | tf_op jit(solution)/shard_map/all_to_all | solution.py:638
  379.3 227.0 %all-gather.26.cloned.1.call-start = ((), (), s32[]{:S(2)}) async-start(), calls=%async_computation.43 | async-start | bytes 11280384 | tf_op jit(solution)/shard_map/all_gather | solution.py:604
  416.3 52.5 %all-to-all-start.5 = ((bf16[4,1024,512]{2,1,0:T(8,128)(2,1)}), bf16[4,1024,512]{2,1,0:T(8,128)(2,1)}, u32[]{:S(2)}, u32[]{:S(2)}) async-start(bf16[4,1024,512]{2,1,0:T(8,128)(2,1)} %pad_maximum_fusion.2), calls=%async_computation.5 | async-start | bytes 8388608 | tf_op jit(solution)/shard_map/all_to_all | solution.py:638
  468.8 47.0 %all-to-all-start.6 = ((bf16[4,1024,128]{2,1,0:T(8,128)(2,1)}), bf16[4,1024,128]{2,1,0:T(8,128)(2,1)S(1)}, u32[]{:S(2)}, u32[]{:S(2)}) async-start(bf16[4,1024,128]{2,1,0:T(8,128)(2,1)} %bitcast.289), calls=%async_computation.6 | async-start | bytes 2097152 | tf_op jit(solution)/shard_map/all_to_all | solution.py:638
  522.8 316.6 %reduce-scatter.10.cloned.1.call-start = ((), (), s32[]{:S(2)}) async-start(), calls=%async_computation.32 | async-start | bytes 11280384 | tf_op jit(solution)/shard_map/reduce_scatter | solution.py:689
  606.2 233.2 %reduce-scatter.12.cloned.1.call-start = ((), (), s32[]{:S(2)}) async-start(), calls=%async_computation.33 | async-start | bytes 10653696 | tf_op jit(solution)/shard_map/reduce_scatter | solution.py:689
  694.4 74.5 %all-to-all-start.9 = ((bf16[4,1024,256]{2,1,0:T(8,128)(2,1)}), bf16[4,1024,256]{2,1,0:T(8,128)(2,1)S(1)}, u32[]{:S(2)}, u32[]{:S(2)}) async-start(bf16[4,1024,256]{2,1,0:T(8,128)(2,1)} %pad_maximum_fusion.6), calls=%async_computation.9 | async-start | bytes 4194304 | tf_op jit(solution)/shard_map/all_to_all | solution.py:638
  769.0 70.5 %all-to-all-start.10 = ((bf16[4,1024,384]{2,1,0:T(8,128)(2,1)}), bf16[4,1024,384]{2,1,0:T(8,128)(2,1)}, u32[]{:S(2)}, u32[]{:S(2)}) async-start(bf16[4,1024,384]{2,1,0:T(8,128)(2,1)} %bitcast.287), calls=%async_computation.10 | async-start | bytes 6291456 | tf_op jit(solution)/shard_map/all_to_all | solution.py:638
  850.1 227.1 %reduce-scatter.14.cloned.1.call-start = ((), (), s32[]{:S(2)}) async-start(), calls=%async_computation.34 | async-start | bytes 10653696 | tf_op jit(solution)/shard_map/reduce_scatter | solution.py:689
  914.8 305.8 %reduce-scatter.16.cloned.1.call-start = ((), (), s32[]{:S(2)}) async-start(), calls=%async_computation.35 | async-start | bytes 11280384 | tf_op jit(solution)/shard_map/reduce_scatter | solution.py:689
  964.1 313.4 %reduce-scatter.18.cloned.1.call-start = ((), (), s32[]{:S(2)}) async-start(), calls=%async_computation.36 | async-start | bytes 10653696 | tf_op jit(solution)/shard_map/reduce_scatter | solution.py:689
  1077.2 73.9 %all-to-all-start.15 = ((bf16[4,1024,256]{2,1,0:T(8,128)(2,1)}), bf16[4,1024,256]{2,1,0:T(8,128)(2,1)S(1)}, u32[]{:S(2)}, u32[]{:S(2)}) async-start(bf16[4,1024,256]{2,1,0:T(8,128)(2,1)} %pad_maximum_fusion.7), calls=%async_computation.18 | async-start | bytes 4194304 | tf_op jit(solution)/shard_map/all_to_all | solution.py:638
  1151.1 69.5 %all-to-all-start.16 = ((bf16[4,1024,384]{2,1,0:T(8,128)(2,1)}), bf16[4,1024,384]{2,1,0:T(8,128)(2,1)}, u32[]{:S(2)}, u32[]{:S(2)}) async-start(bf16[4,1024,384]{2,1,0:T(8,128)(2,1)} %bitcast.286), calls=%async_computation.19 | async-start | bytes 6291456 | tf_op jit(solution)/shard_map/all_to_all | solution.py:638
  1155.9 134.8 %reduce-scatter.22.cloned.1.call-start = ((), (), s32[]{:S(2)}) async-start(), calls=%async_computation.44 | async-start | bytes 2820096
  1231.3 213.1 %reduce-scatter.20.cloned.1.call-start = ((), (), s32[]{:S(2)}) async-start(), calls=%async_computation.37 | async-start | bytes 8146944 | tf_op jit(solution)/shard_map/reduce_scatter | solution.py:689
  1314.1 47.2 %all-to-all-start.18 = ((bf16[4,408,1088]{2,1,0:T(8,128)(2,1)}), bf16[4,408,1088]{2,1,0:T(8,128)(2,1)}, u32[]{:S(2)}, u32[]{:S(2)}) async-start(bf16[4,408,1088]{2,1,0:T(8,128)(2,1)} %pad_maximum_fusion.3), calls=%async_computation.23 | async-start | bytes 7520256 | tf_op jit(solution)/shard_map/all_to_all | solution.py:638
  1366.7 47.4 %all-to-all-start.19 = ((bf16[4,408,1088]{2,1,0:T(8,128)(2,1)}), bf16[4,408,1088]{2,1,0:T(8,128)(2,1)}, u32[]{:S(2)}, u32[]{:S(2)}) async-start(bf16[4,408,1088]{2,1,0:T(8,128)(2,1)} %broadcast_in_dim.48), calls=%async_computation.24 | async-start | bytes 7520256 | tf_op jit(solution)/shard_map/all_to_all | solution.py:638
  (153 other events, 3243.9 us)
Sparse Core Ops, SparseCore 0:
  9.7 48.8 all-gather.15
  60.8 89.6 all-gather.17
  152.7 94.0 all-gather.19
  248.9 70.9 all-gather.13
  321.4 31.4 all-gather.21
  354.4 90.0 all-gather.23
  446.7 94.0 all-gather.25
  606.3 111.3 reduce-scatter.9
  720.0 98.4 reduce-scatter.11
  914.9 97.2 reduce-scatter.13
  1014.6 103.4 reduce-scatter.15
  1120.2 98.4 reduce-scatter.17
  1221.0 37.0 reduce-scatter.21
  1290.8 76.2 reduce-scatter.19
